TPU v7x, 512 devices: a whole 4x8x8 slice. The times are simulated.
512 devices in a mesh: seq: 128 (over y, z, core), blk: 4 (over x).
Axes of the slice: x: 4, y: 8, z: 8, core: 2. Of those that a mesh axis runs over, the one named last changes fastest.
Arguments:
- queries: bfloat16 [65536, 4096], P(('seq', 'blk')), may hold values from -24 to 24
- keys: bfloat16 [65536, 4096], P(('seq', 'blk')), may hold values from -24 to 24
- values: bfloat16 [65536, 4096], P(('seq', 'blk')), may hold values from -6 to 6
- cluster_ids: int32 [65536, 1], P(('seq', 'blk')), may hold values from 0 to 127; in each aligned block of 128 rows (0 to 127, 128 to 255, ...) at most 2 rows name the same one
Outputs:
- attended: bfloat16 [65536, 4096], P(('seq', 'blk'))
Inputs may be any that keep to these rules, and one draw needn't show every extreme that they name: `cluster_ids`: at most 2 tokens of one device share a cluster, and that many are reached.
All inputs are finite; a program needn't handle non-finite values.
Results may differ from a plain program's by a relative error of at most 0.0085.
Values may be sent and summed in bfloat16 or wider, within the bound.
No kernel may reach another device: no remote copies, remote signals or barrier semaphores. Data moves between devices by JAX's collectives and lax.ppermute only.
A program may use at most 64 MiB of HBM per device.

v0:
```python
import jax
import jax.numpy as jnp
from jax import lax
from jax.sharding import PartitionSpec as P

HEADS = 32


def owner_slots(cluster, owners, capacity):
    onehot = (cluster[:, None] == jnp.arange(owners, dtype=jnp.int32)[None, :]).astype(jnp.int32)
    earlier = jnp.cumsum(onehot, axis=0) - onehot
    within = jnp.sum(earlier * onehot, axis=1)
    return cluster * capacity + within


def attend(queries, keys, values, places, heads):
    rows = queries.shape[0]
    width = queries.shape[1] // heads
    scale = 1.0 / width**0.5
    valid = places >= 0
    allowed = (places[None, :] <= places[:, None]) & valid[None, :]

    def one_head(index):
        start = index * width
        q_head = lax.dynamic_slice_in_dim(queries, start, width, 1)
        k_head = lax.dynamic_slice_in_dim(keys, start, width, 1)
        v_head = lax.dynamic_slice_in_dim(values, start, width, 1)
        scores = (
            lax.dot_general(
                q_head, k_head, (((1,), (1,)), ((), ())), preferred_element_type=jnp.float32
            )
            * scale
        )
        scores = jnp.where(allowed, scores, -1e30)
        top = jnp.max(scores, axis=1, keepdims=True)
        weights = jnp.where(allowed, jnp.exp(scores - top), 0.0)
        total = jnp.sum(weights, axis=1, keepdims=True)
        mixed = (
            jnp.dot(weights.astype(jnp.bfloat16), v_head, preferred_element_type=jnp.float32)
            / total
        )
        return mixed.astype(jnp.bfloat16)

    stacked = lax.map(one_head, jnp.arange(heads, dtype=jnp.int32))
    return jnp.transpose(stacked, (1, 0, 2)).reshape(rows, heads * width)


def body(queries, keys, values, cluster_ids):
    count = queries.shape[0]
    width_all = queries.shape[1]
    seq_count = lax.axis_size("seq")
    blk_count = lax.axis_size("blk")
    head_share = HEADS // blk_count
    piece = width_all // blk_count
    most = 2 * count // seq_count
    cluster = cluster_ids[:, 0]
    first = (lax.axis_index("seq") * blk_count + lax.axis_index("blk")) * count
    places = first + jnp.arange(count, dtype=jnp.int32)
    slots = owner_slots(cluster, seq_count, most)
    rows_out = seq_count * most

    def place(data):
        return jnp.zeros((rows_out, width_all), data.dtype).at[slots].set(data)

    sent_places = jnp.full((rows_out,), -1, dtype=jnp.int32).at[slots].set(places)
    got_q, got_k, got_v, got_p = (
        lax.all_to_all(place(queries), "seq", split_axis=0, concat_axis=0, tiled=True),
        lax.all_to_all(place(keys), "seq", split_axis=0, concat_axis=0, tiled=True),
        lax.all_to_all(place(values), "seq", split_axis=0, concat_axis=0, tiled=True),
        lax.all_to_all(sent_places, "seq", split_axis=0, concat_axis=0, tiled=True),
    )
    spread_p = jnp.broadcast_to(got_p[:, None, None], (rows_out, blk_count, 1))
    part_q, part_k, part_v, part_p = (
        lax.all_to_all(
            got_q.reshape(rows_out, blk_count, piece),
            "blk",
            split_axis=1,
            concat_axis=0,
            tiled=True,
        ),
        lax.all_to_all(
            got_k.reshape(rows_out, blk_count, piece),
            "blk",
            split_axis=1,
            concat_axis=0,
            tiled=True,
        ),
        lax.all_to_all(
            got_v.reshape(rows_out, blk_count, piece),
            "blk",
            split_axis=1,
            concat_axis=0,
            tiled=True,
        ),
        lax.all_to_all(spread_p, "blk", split_axis=1, concat_axis=0, tiled=True),
    )
    total_rows = blk_count * rows_out
    mixed = attend(
        part_q.reshape(total_rows, piece),
        part_k.reshape(total_rows, piece),
        part_v.reshape(total_rows, piece),
        part_p.reshape(total_rows),
        head_share,
    )
    joined = lax.all_to_all(
        mixed.reshape(total_rows, 1, piece), "blk", split_axis=0, concat_axis=1, tiled=True
    )
    back = lax.all_to_all(
        joined.reshape(rows_out, width_all), "seq", split_axis=0, concat_axis=0, tiled=True
    )
    return back[slots]


def solution(mesh):
    return jax.shard_map(
        body,
        mesh=mesh,
        in_specs=(
            P(("seq", "blk"), None),
            P(("seq", "blk"), None),
            P(("seq", "blk"), None),
            P(("seq", "blk"), None),
        ),
        out_specs=P(("seq", "blk"), None),
        check_vma=False,
    )
```

profile of v0, /device:TPU:1, one launch (start us, length us, event | category | flops | bytes accessed | tf_op | source)
XLA Modules:
  0.0 503.1 jit_solution(18135439097035509343)
XLA Ops:
  3.5 29.7 %all_to_all.123 = s32[128,2,1]{1,2,0:T(1,128)S(1)} all-to-all(s32[128,2,1]{1,2,0:T(1,128)S(1)} %bitcast.52), channel_id=1, replica_groups=mesh['seq'=128,'blk'=4] {'seq'}, dimensions={0} | all-to-all | bytes 2048 | tf_op jit(solution)/shard_map/all_to_all | solution.py:70
  35.4 4.0 all-to-all-start.5
  39.4 3.4 scatter_custom_fusion.3
  42.8 2.7 all_to_all.102
  45.5 6.0 %all-to-all-start.6 = ((bf16[128,2,4096]{2,1,0:T(2,128)(2,1)}), bf16[128,2,4096]{2,1,0:T(2,128)(2,1)S(1)}, u32[]{:S(2)}, u32[]{:S(2)}) async-start(bf16[128,2,4096]{2,1,0:T(2,128)(2,1)} %all_to_all.102), calls=%async_computation.6 | async-start | bytes 4194304 | tf_op jit(solution)/shard_map/all_to_all | solution.py:69
  51.5 4.3 scatter_custom_fusion
  55.8 4.4 all_to_all.87
  60.2 43.5 %all-to-all-done.6 = bf16[128,2,4096]{2,1,0:T(2,128)(2,1)S(1)} async-done(((bf16[128,2,4096]{2,1,0:T(2,128)(2,1)}), bf16[128,2,4096]{2,1,0:T(2,128)(2,1)S(1)}, u32[]{:S(2)}, u32[]{:S(2)}) %all-to-all-start.6) | async-done | bytes 2097184 | tf_op jit(solution)/shard_map/all_to_all | solution.py:69
  103.8 1.3 copy-done
  105.1 7.8 %all-to-all-start = ((bf16[128,2,4096]{2,1,0:T(2,128)(2,1)}), bf16[128,2,4096]{2,1,0:T(2,128)(2,1)S(1)}, u32[]{:S(2)}, u32[]{:S(2)}) async-start(bf16[128,2,4096]{2,1,0:T(2,128)(2,1)} %all_to_all.87), calls=%async_computation | async-start | bytes 4194304 | tf_op jit(solution)/shard_map/all_to_all | solution.py:67
  112.9 4.3 scatter_custom_fusion.1
  117.2 4.4 all_to_all.92
  121.6 43.4 %all-to-all-done = bf16[128,2,4096]{2,1,0:T(2,128)(2,1)S(1)} async-done(((bf16[128,2,4096]{2,1,0:T(2,128)(2,1)}), bf16[128,2,4096]{2,1,0:T(2,128)(2,1)S(1)}, u32[]{:S(2)}, u32[]{:S(2)}) %all-to-all-start) | async-done | bytes 2097184 | tf_op jit(solution)/shard_map/all_to_all | solution.py:67
  165.1 8.2 %all-to-all-start.2 = ((bf16[128,2,4096]{2,1,0:T(2,128)(2,1)}), bf16[128,2,4096]{2,1,0:T(2,128)(2,1)}, u32[]{:S(2)}, u32[]{:S(2)}) async-start(bf16[128,2,4096]{2,1,0:T(2,128)(2,1)} %all_to_all.92), calls=%async_computation.2 | async-start | bytes 4194304 | tf_op jit(solution)/shard_map/all_to_all | solution.py:68
  173.3 4.4 reshape.61
  177.7 3.5 copy.15
  181.3 43.8 %all-to-all-done.2 = bf16[128,2,4096]{2,1,0:T(2,128)(2,1)} async-done(((bf16[128,2,4096]{2,1,0:T(2,128)(2,1)}), bf16[128,2,4096]{2,1,0:T(2,128)(2,1)}, u32[]{:S(2)}, u32[]{:S(2)}) %all-to-all-start.2) | async-done | bytes 2097184 | tf_op jit(solution)/shard_map/all_to_all | solution.py:68
  225.1 4.5 all-to-all-start.7
  229.6 2.7 reshape.57
  232.3 3.6 copy.13
  235.9 19.7 %all-to-all-done.7 = bf16[256,4,1024]{2,0,1:T(8,128)(2,1)} async-done(((bf16[256,4,1024]{2,0,1:T(8,128)(2,1)}), bf16[256,4,1024]{2,0,1:T(8,128)(2,1)}, u32[]{:S(2)}, u32[]{:S(2)}) %all-to-all-start.7) | async-done | bytes 2097184 | tf_op jit(solution)/shard_map/all_to_all | solution.py:88
  255.6 4.4 all-to-all-start.1
  260.0 3.2 reshape.59
  263.2 2.0 copy.14
  265.2 19.6 %all-to-all-done.1 = bf16[256,4,1024]{2,0,1:T(8,128)(2,1)} async-done(((bf16[256,4,1024]{2,0,1:T(8,128)(2,1)}), bf16[256,4,1024]{2,0,1:T(8,128)(2,1)}, u32[]{:S(2)}, u32[]{:S(2)}) %all-to-all-start.1) | async-done | bytes 2097184 | tf_op jit(solution)/shard_map/all_to_all | solution.py:74
  284.8 3.8 all-to-all-start.3
  288.7 23.5 %all-to-all-done.3 = bf16[256,4,1024]{2,0,1:T(8,128)(2,1)S(1)} async-done(((bf16[256,4,1024]{2,0,1:T(8,128)(2,1)}), bf16[256,4,1024]{2,0,1:T(8,128)(2,1)S(1)}, u32[]{:S(2)}, u32[]{:S(2)}) %all-to-all-start.3) | async-done | bytes 2097184 | tf_op jit(solution)/shard_map/all_to_all | solution.py:81
  312.2 70.7 %while.11 = (s32[]{:T(128)}, bf16[8,1024,128]{1,2,0:T(8,128)(2,1)}, s32[8]{0:T(128)S(1)}, bf16[1024,1024]{1,0:T(8,128)(2,1)}, bf16[1024,1024]{1,0:T(8,128)(2,1)S...) while((s32[]{:T(128)}, bf16[8,1024,128]{1,2,0:T(8,128)(2,1)}, ...), condition=%wide.region_9.10_spmd.clone, body=%wide.region_6.9_spmd.clone.sunk | while | flops 557053952 | bytes 14725811 | solution.py:44
  313.4 2.1 fusion.38
  315.5 1.9 fusion.39
  317.4 2.8 fusion.40
  322.2 2.1 fusion.38
  324.3 1.9 fusion.39
  326.2 2.8 fusion.40
  331.0 2.1 fusion.38
  333.2 1.9 fusion.39
  335.0 2.8 fusion.40
  339.9 2.1 fusion.38
  342.0 1.9 fusion.39
  343.9 2.8 fusion.40
  348.7 2.1 fusion.38
  350.8 1.9 fusion.39
  352.7 2.8 fusion.40
  357.6 2.1 fusion.38
  359.7 1.9 fusion.39
  361.5 2.8 fusion.40
  366.4 2.1 fusion.38
  368.5 1.9 fusion.39
  370.4 2.8 fusion.40
  375.2 2.1 fusion.38
  377.4 1.9 fusion.39
  379.2 2.8 fusion.40
  383.4 3.9 reduce.4
  387.3 2.6 copy.27
  389.9 4.5 reshape.120
  394.4 26.2 %all_to_all.124 = bf16[4,2,131072]{2,1,0:T(2,128)(2,1)S(1)} all-to-all(bf16[4,2,131072]{2,1,0:T(2,128)(2,1)} %reshape.120), channel_id=1, replica_groups=mesh['seq'=128,'blk'=4] {'blk'}, dimensions={0} | all-to-all | bytes 4194304 | tf_op jit(solution)/shard_map/all_to_all | solution.py:105
  420.6 3.4 reshape.121
  423.9 3.0 copy.23
  426.9 1.6 copy.19
  428.6 2.7 all_to_all.110
  431.2 15.1 %all-to-all-start.9 = ((bf16[128,2,4096]{2,1,0:T(2,128)(2,1)}), bf16[128,2,4096]{2,1,0:T(2,128)(2,1)}, u32[]{:S(2)}, u32[]{:S(2)}) async-start(bf16[128,2,4096]{2,1,0:T(2,128)(2,1)} %all_to_all.110), calls=%async_computation.9 | async-start | bytes 4194304 | tf_op jit(solution)/shard_map/all_to_all | solution.py:108
  446.4 51.8 %all-to-all-done.9 = bf16[128,2,4096]{2,1,0:T(2,128)(2,1)} async-done(((bf16[128,2,4096]{2,1,0:T(2,128)(2,1)}), bf16[128,2,4096]{2,1,0:T(2,128)(2,1)}, u32[]{:S(2)}, u32[]{:S(2)}) %all-to-all-start.9) | async-done | bytes 2097184 | tf_op jit(solution)/shard_map/all_to_all | solution.py:108
  498.1 2.7 all_to_all.112
  500.9 2.2 gather_fusion
  (44 shorter events, 17.8 us)
Async XLA Ops:
  35.4 10.1 %all-to-all-start.5 = ((s32[256,4,1]{0,2,1:T(1,128)}), s32[256,4,1]{0,2,1:T(1,128)S(1)}, u32[]{:S(2)}, u32[]{:S(2)}) async-start(s32[256,4,1]{0,2,1:T(1,128)} %broadcast_in_dim.37), calls=%async_computation.5 | async-start | bytes 8192 | tf_op jit(solution)/shard_map/all_to_all | solution.py:95
  45.5 58.3 %all-to-all-start.6 = ((bf16[128,2,4096]{2,1,0:T(2,128)(2,1)}), bf16[128,2,4096]{2,1,0:T(2,128)(2,1)S(1)}, u32[]{:S(2)}, u32[]{:S(2)}) async-start(bf16[128,2,4096]{2,1,0:T(2,128)(2,1)} %all_to_all.102), calls=%async_computation.6 | async-start | bytes 4194304 | tf_op jit(solution)/shard_map/all_to_all | solution.py:69
  103.8 1.3 copy-start
  105.1 59.9 %all-to-all-start = ((bf16[128,2,4096]{2,1,0:T(2,128)(2,1)}), bf16[128,2,4096]{2,1,0:T(2,128)(2,1)S(1)}, u32[]{:S(2)}, u32[]{:S(2)}) async-start(bf16[128,2,4096]{2,1,0:T(2,128)(2,1)} %all_to_all.87), calls=%async_computation | async-start | bytes 4194304 | tf_op jit(solution)/shard_map/all_to_all | solution.py:67
  165.1 60.0 %all-to-all-start.2 = ((bf16[128,2,4096]{2,1,0:T(2,128)(2,1)}), bf16[128,2,4096]{2,1,0:T(2,128)(2,1)}, u32[]{:S(2)}, u32[]{:S(2)}) async-start(bf16[128,2,4096]{2,1,0:T(2,128)(2,1)} %all_to_all.92), calls=%async_computation.2 | async-start | bytes 4194304 | tf_op jit(solution)/shard_map/all_to_all | solution.py:68
  225.1 30.5 %all-to-all-start.7 = ((bf16[256,4,1024]{2,0,1:T(8,128)(2,1)}), bf16[256,4,1024]{2,0,1:T(8,128)(2,1)}, u32[]{:S(2)}, u32[]{:S(2)}) async-start(bf16[256,4,1024]{2,0,1:T(8,128)(2,1)} %copy.15), calls=%async_computation.7 | async-start | bytes 4194304 | tf_op jit(solution)/shard_map/all_to_all | solution.py:88
  255.6 29.2 %all-to-all-start.1 = ((bf16[256,4,1024]{2,0,1:T(8,128)(2,1)}), bf16[256,4,1024]{2,0,1:T(8,128)(2,1)}, u32[]{:S(2)}, u32[]{:S(2)}) async-start(bf16[256,4,1024]{2,0,1:T(8,128)(2,1)} %copy.13), calls=%async_computation.1 | async-start | bytes 4194304 | tf_op jit(solution)/shard_map/all_to_all | solution.py:74
  284.8 27.4 %all-to-all-start.3 = ((bf16[256,4,1024]{2,0,1:T(8,128)(2,1)}), bf16[256,4,1024]{2,0,1:T(8,128)(2,1)S(1)}, u32[]{:S(2)}, u32[]{:S(2)}) async-start(bf16[256,4,1024]{2,0,1:T(8,128)(2,1)} %copy.14), calls=%async_computation.3 | async-start | bytes 4194304 | tf_op jit(solution)/shard_map/all_to_all | solution.py:81
  431.2 66.9 %all-to-all-start.9 = ((bf16[128,2,4096]{2,1,0:T(2,128)(2,1)}), bf16[128,2,4096]{2,1,0:T(2,128)(2,1)}, u32[]{:S(2)}, u32[]{:S(2)}) async-start(bf16[128,2,4096]{2,1,0:T(2,128)(2,1)} %all_to_all.110), calls=%async_computation.9 | async-start | bytes 4194304 | tf_op jit(solution)/shard_map/all_to_all | solution.py:108
where the time goes:
time: 505 us; the launch traced here: 503 us
  waiting for transfers between devices  245 us (49%)
  local copies, waits for them, and re-layouts  81.4 us (16%)
  blocking collectives  55.9 us (11%)
  starting transfers between devices  54 us (11%)
  matrix products  39.2 us (8%)
  other arithmetic  22 us (4%)
    all_to_all x1, waiting for transfers between devices, body(): lax.all_to_all(joined.reshape(rows_out, width_all), 'seq', split_axis=0,...  51.8 us
    all_to_all x1, waiting for transfers between devices, body(): lax.all_to_all(place(keys), 'seq', split_axis=0, concat_axis=0, tiled=True)  43.8 us
    all_to_all x1, waiting for transfers between devices, body(): lax.all_to_all(place(values), 'seq', split_axis=0, concat_axis=0, tiled=T...  43.5 us
    all_to_all x1, waiting for transfers between devices, body(): lax.all_to_all(place(queries), 'seq', split_axis=0, concat_axis=0, tiled=...  43.4 us
    all_to_all x1, blocking collectives, body(): lax.all_to_all(sent_places, 'seq', split_axis=0, concat_axis=0, tiled=True)  29.7 us
    all_to_all x1, blocking collectives, body(): lax.all_to_all(mixed.reshape(total_rows, 1, piece), 'blk', split_axis=0,...  26.2 us
    all_to_all x1, waiting for transfers between devices, body(): lax.all_to_all(got_k.reshape(rows_out, blk_count, piece), 'blk', split_ax...  23.5 us
    dot_general x8, matrix products, one_head(): jnp.dot(weights.astype(jnp.bfloat16), v_head, preferred_element_type=jnp....  22.3 us
  transfers between devices with their start and end apart: 8, of which 7 were waited for; matrix products, arithmetic and copies ran while one was open for 6% of the time, Pallas kernels for 0%

commit v1 on v0

v1 whole, which is shorter than its diff:
```python
import jax
import jax.numpy as jnp
from jax import lax
from jax.experimental import pallas as pl
from jax.experimental.pallas import tpu as pltpu
from jax.sharding import PartitionSpec as P

HEADS = 32
HEAD = 128
TOK = 128
CLUSTERS = 128
MOST = 2
GROUPS = 4
SHARE = HEADS // GROUPS
UNIT = SHARE * MOST
DEVICES = CLUSTERS * GROUPS
ROWS = DEVICES * MOST
QBLK = 256
EMPTY = 256.0
MASKED = -1e30
FACTOR = 1.4426950408889634 / HEAD**0.5
BF16 = jnp.bfloat16
F32 = jnp.float32


def iota(shape, dim):
    return lax.broadcasted_iota(jnp.int32, shape, dim)


def swap_matrix():
    size = SHARE * UNIT
    out, src = iota((size, size), 0), iota((size, size), 1)
    a, b, s = out // UNIT, (out // MOST) % SHARE, out % MOST
    return (src == b * UNIT + a * MOST + s).astype(F32).astype(BF16)


def slot_row(col, row):
    same = (col == row) & (iota((TOK, TOK), 0) < iota((TOK, TOK), 1))
    within = jnp.sum(same.astype(F32), axis=0, keepdims=True)
    return row.astype(F32) * MOST + within


def dot(a, b):
    return jnp.dot(a, b, preferred_element_type=F32)


def pack_kernel(col_ref, row_ref, q_ref, k_ref, v_ref, out_ref):
    slots = slot_row(col_ref[...], row_ref[...])
    numbers = iota((CLUSTERS * MOST, TOK), 0).astype(F32)
    onehot = (numbers == slots).astype(F32)
    filled = jnp.sum(onehot, axis=1, keepdims=True) > 0.5
    onehot = onehot.astype(BF16)
    first_lane = (iota((CLUSTERS * MOST, SHARE * HEAD), 1) % HEAD) == 0
    swap = swap_matrix()
    for index, ref in enumerate((q_ref, k_ref, v_ref)):
        rows = dot(onehot, ref[...])
        if index == 1:
            rows = jnp.where(first_lane & jnp.logical_not(filled), EMPTY, rows)
        rows = rows.astype(BF16)
        for block in range(CLUSTERS // SHARE):
            part = rows[block * UNIT : (block + 1) * UNIT, :]
            tall = jnp.concatenate(
                [part[:, h * HEAD : (h + 1) * HEAD] for h in range(SHARE)], axis=0
            )
            mixed = dot(swap, tall).astype(BF16)
            out_ref[
                block * SHARE : (block + 1) * SHARE, 0, index * UNIT : (index + 1) * UNIT, :
            ] = mixed.reshape(SHARE, UNIT, HEAD)


def pack(col, row, queries, keys, values):
    data = pl.BlockSpec((TOK, SHARE * HEAD), lambda g: (0, g))
    return pl.pallas_call(
        pack_kernel,
        grid=(GROUPS,),
        in_specs=[
            pl.BlockSpec((TOK, 1), lambda g: (0, 0)),
            pl.BlockSpec((1, TOK), lambda g: (0, 0)),
            data,
            data,
            data,
        ],
        out_specs=pl.BlockSpec((CLUSTERS, 1, 3 * UNIT, HEAD), lambda g: (0, g, 0, 0)),
        out_shape=jax.ShapeDtypeStruct((CLUSTERS, GROUPS, 3 * UNIT, HEAD), BF16),
        compiler_params=pltpu.CompilerParams(vmem_limit_bytes=32 * 1024 * 1024),
        name="pack",
    )(col, row, queries, keys, values)


def attend_kernel(in_ref, out_ref, q_scr, k_scr, v_scr, o_scr, bias_scr):
    swap = swap_matrix()

    def regroup(block, carry):
        first = pl.multiple_of(block * SHARE, SHARE)
        start = pl.multiple_of(block * UNIT, UNIT)
        part = in_ref[pl.ds(first, SHARE), :, :]
        for index, ref in enumerate((q_scr, k_scr, v_scr)):
            tall = part[:, index * UNIT : (index + 1) * UNIT, :].reshape(SHARE * UNIT, HEAD)
            mixed = dot(swap, tall).astype(BF16)
            ref[:, pl.ds(start, UNIT), :] = mixed.reshape(SHARE, UNIT, HEAD)
        return carry

    lax.fori_loop(0, DEVICES // SHARE, regroup, 0, unroll=4)

    pick = (iota((8, HEAD), 1) == 0).astype(F32).astype(BF16)
    marks = lax.dot_general(
        pick, k_scr[0], (((1,), (1,)), ((), ())), preferred_element_type=F32
    )
    bias_scr[...] = jnp.where(marks > EMPTY / 2, MASKED, 0.0)

    def one_head(h, carry):
        for block in range(ROWS // QBLK):
            start, stop = block * QBLK, (block + 1) * QBLK
            q = q_scr[h, start:stop, :]
            k = k_scr[h, 0:stop, :]
            v = v_scr[h, 0:stop, :]
            scores = lax.dot_general(
                q, k, (((1,), (1,)), ((), ())), preferred_element_type=F32
            )
            scores = scores + bias_scr[0:1, 0:stop]
            later = iota((QBLK, QBLK), 1) > iota((QBLK, QBLK), 0)
            last = jnp.where(later, MASKED, scores[:, start:stop])
            if block:
                scores = jnp.concatenate([scores[:, :start], last], axis=1)
            else:
                scores = last
            top = jnp.max(scores, axis=1, keepdims=True)
            weights = jnp.exp2((scores - top) * FACTOR)
            total = jnp.sum(weights, axis=1, keepdims=True)
            mixed = dot(weights.astype(BF16), v) / total
            o_scr[h, start:stop, :] = mixed.astype(BF16)
        return carry

    lax.fori_loop(0, SHARE, one_head, 0)

    def ungroup(block, carry):
        first = pl.multiple_of(block * SHARE, SHARE)
        start = pl.multiple_of(block * UNIT, UNIT)
        tall = o_scr[:, pl.ds(start, UNIT), :].reshape(SHARE * UNIT, HEAD)
        mixed = dot(swap, tall).astype(BF16)
        out_ref[pl.ds(first, SHARE), :, :] = mixed.reshape(SHARE, UNIT, HEAD)
        return carry

    lax.fori_loop(0, DEVICES // SHARE, ungroup, 0, unroll=4)


def attend(received):
    held = pltpu.VMEM((SHARE, ROWS, HEAD), BF16)
    return pl.pallas_call(
        attend_kernel,
        in_specs=[pl.BlockSpec(memory_space=pltpu.VMEM)],
        out_specs=pl.BlockSpec(memory_space=pltpu.VMEM),
        out_shape=jax.ShapeDtypeStruct((DEVICES, UNIT, HEAD), BF16),
        scratch_shapes=[held, held, held, held, pltpu.VMEM((8, ROWS), F32)],
        compiler_params=pltpu.CompilerParams(vmem_limit_bytes=48 * 1024 * 1024),
        name="attend",
    )(received)


def unpack_kernel(col_ref, row_ref, in_ref, out_ref):
    slots = slot_row(col_ref[...], row_ref[...])
    numbers = iota((CLUSTERS * MOST, TOK), 0).astype(F32)
    onehot = (numbers == slots).astype(F32).astype(BF16)
    swap = swap_matrix()
    blocks = []
    for block in range(CLUSTERS // SHARE):
        tall = in_ref[block * SHARE : (block + 1) * SHARE, 0, :, :].reshape(SHARE * UNIT, HEAD)
        mixed = dot(swap, tall).astype(BF16)
        blocks.append(
            jnp.concatenate([mixed[h * UNIT : (h + 1) * UNIT, :] for h in range(SHARE)], axis=1)
        )
    rows = jnp.concatenate(blocks, axis=0)
    out_ref[...] = lax.dot_general(
        onehot, rows, (((0,), (0,)), ((), ())), preferred_element_type=F32
    ).astype(BF16)


def unpack(col, row, back):
    return pl.pallas_call(
        unpack_kernel,
        grid=(GROUPS,),
        in_specs=[
            pl.BlockSpec((TOK, 1), lambda g: (0, 0)),
            pl.BlockSpec((1, TOK), lambda g: (0, 0)),
            pl.BlockSpec((CLUSTERS, 1, UNIT, HEAD), lambda g: (0, g, 0, 0)),
        ],
        out_specs=pl.BlockSpec((TOK, SHARE * HEAD), lambda g: (0, g)),
        out_shape=jax.ShapeDtypeStruct((TOK, HEADS * HEAD), BF16),
        compiler_params=pltpu.CompilerParams(vmem_limit_bytes=32 * 1024 * 1024),
        name="unpack",
    )(col, row, back)


def exchange(data):
    return lax.all_to_all(data, ("seq", "blk"), split_axis=0, concat_axis=0, tiled=True)


def body(queries, keys, values, cluster_ids):
    row = cluster_ids.reshape(1, TOK)
    sent = pack(cluster_ids, row, queries, keys, values)
    received = exchange(sent.reshape(DEVICES, 3 * UNIT, HEAD))
    mixed = attend(received)
    back = exchange(mixed)
    return unpack(cluster_ids, row, back.reshape(CLUSTERS, GROUPS, UNIT, HEAD))


def solution(mesh):
    spec = P(("seq", "blk"), None)
    return jax.shard_map(
        body, mesh=mesh, in_specs=(spec,) * 4, out_specs=spec, check_vma=False
    )
```

time: 505 us -> 267 us (0.53)
  waiting for transfers between devices: 245 us -> 0 us
  blocking collectives: 55.9 us -> 229 us
  local copies, waits for them, and re-layouts: 81.4 us -> 5.09 us
  starting transfers between devices: 54 us -> 0 us
  matrix products: 39.2 us -> 0 us
  Pallas kernels: 0 us -> 32.5 us
  other arithmetic: 22 us -> 0 us
    all_to_all x8 -> x0, waiting for transfers between devices: 245 us -> none  [the longest x1 51.8 us: body(): lax.all_to_all(joined.reshape(rows_out, width_all), 'seq', split_axis=0,...]
    all_to_all x2, blocking collectives: 55.9 us -> 229 us  [exchange(): lax.all_to_all(data, ('seq', 'blk'), split_axis=0, concat_axis=0, tiled=T...]
    all_to_all x8 -> x0, starting transfers between devices: 54 us -> none  [the longest x1 15.1 us: body(): lax.all_to_all(joined.reshape(rows_out, width_all), 'seq', split_axis=0,...]
    dot_general x16 -> x0, matrix products: 39.2 us -> none  [the longest x8 22.3 us: one_head(): jnp.dot(weights.astype(jnp.bfloat16), v_head, preferred_element_type=jnp....]
    pallas_call x0 -> x3, Pallas kernels: none -> 32.5 us  [the longest x1 23.5 us: attend(): pl.pallas_call(attend_kernel, in_specs=[pl.BlockSpec(memory_space=pltpu.V...]
    reshape x6 -> x0, local copies, waits for them, and re-layouts: 19.4 us -> none  [the longest x2 7.94 us: body(): got_v.reshape(rows_out, blk_count, piece)]
    all_to_all x8 -> x0, local copies, waits for them, and re-layouts: 19.1 us -> none  [the longest x2 5.4 us: body(): lax.all_to_all(joined.reshape(rows_out, width_all), 'seq', split_axis=0,...]
    reduce_sum x9 -> x0, other arithmetic: 15.6 us -> none  [the longest x8 14.8 us: one_head(): total = jnp.sum(weights, axis=1, keepdims=True)]
  transfers between devices with their start and end apart: 8 -> 0, of which waited for: 7 -> 0; matrix products, arithmetic and copies ran while one was open for 6% -> 0% of each run, Pallas kernels for 0% -> 0%
where the time goes in v1:
time: 267 us
  blocking collectives  229 us (86%)
  Pallas kernels  32.5 us (12%)
  local copies, waits for them, and re-layouts  5.09 us (2%)
    all_to_all x2, blocking collectives, exchange(): lax.all_to_all(data, ('seq', 'blk'), split_axis=0, concat_axis=0, tiled=T...  229 us
    pallas_call x1, Pallas kernels, attend(): pl.pallas_call(attend_kernel, in_specs=[pl.BlockSpec(memory_space=pltpu.V...  23.5 us
    pallas_call x1, Pallas kernels, pack(): pl.pallas_call(pack_kernel, grid=(GROUPS,), in_specs=[pl.BlockSpec((TOK,...  5.9 us

profile of v1, /device:TPU:1, one launch (start us, length us, event | category | flops | bytes accessed | tf_op | source)
XLA Modules:
  0.0 267.1 jit_solution(16649561564024273928)
XLA Ops:
  0.0 0.8 copy.6.col_ref
  0.8 0.0 copy-start
  0.8 1.2 copy-done
  2.0 0.0 copy-start.1
  2.0 1.2 copy-done.1
  3.2 0.0 copy-start.2
  3.2 1.2 copy-done.2
  4.4 0.0 copy-start.3
  4.4 0.7 copy-done.3
  5.1 5.9 %pack.1 = bf16[128,4,48,128]{3,2,1,0:T(8,128)(2,1)S(1)} custom-call(s32[128,1]{1,0:T(8,128)S(1)} %copy.6.col_ref, s32[1,128]{1,0:T(1,128)S(1)} %bitcast.5, bf16[128,4096]{1,0:T(8,128)(2,1)S(1)} %copy-done, bf16[128,4096]{1,0:T(8,128)(2,1)S(1)} %copy-done.1, bf16[128,4096]{1,0:T(8,128)(2,1)S(1)} %copy-done.2), custom_call_target="tpu_custom_call" | custom-call | tf_op jit(solution)/shard_map/pack/pallas_call | solution.py:73
  11.0 164.2 %all_to_all.10.in_ref = bf16[512,48,128]{2,1,0:T(8,128)(2,1)} all-to-all(bf16[512,48,128]{2,1,0:T(8,128)(2,1)S(1)} %bitcast.3), channel_id=1, replica_groups=mesh['seq'=128,'blk'=4] {'seq','blk'}, dimensions={0} | all-to-all | bytes 12582912 | tf_op jit(solution)/shard_map/all_to_all | solution.py:195
  175.2 0.0 copy-start.4
  175.2 23.5 %attend.1 = bf16[512,16,128]{2,1,0:T(8,128)(2,1)S(1)} custom-call(bf16[512,48,128]{2,1,0:T(8,128)(2,1)} %all_to_all.10.in_ref), custom_call_target="tpu_custom_call" | custom-call | tf_op jit(solution)/shard_map/attend/pallas_call | solution.py:149
  198.8 65.2 %all_to_all.11 = bf16[512,16,128]{2,1,0:T(8,128)(2,1)S(1)} all-to-all(bf16[512,16,128]{2,1,0:T(8,128)(2,1)S(1)} %attend.1), channel_id=1, replica_groups=mesh['seq'=128,'blk'=4] {'seq','blk'}, dimensions={0} | all-to-all | bytes 4194304 | tf_op jit(solution)/shard_map/all_to_all | solution.py:195
  264.0 0.0 copy-done.4
  264.0 3.1 %unpack.1 = bf16[128,4096]{1,0:T(8,128)(2,1)} custom-call(s32[128,1]{1,0:T(8,128)S(1)} %copy.6.col_ref, s32[1,128]{1,0:T(1,128)S(1)} %bitcast.6, bf16[128,4,16,128]{3,2,1,0:T(8,128)(2,1)S(1)} %bitcast.4), custom_call_target="tpu_custom_call" | custom-call | tf_op jit(solution)/shard_map/unpack/pallas_call | solution.py:179
Async XLA Ops:
  0.8 1.2 copy-start
  2.0 1.2 copy-start.1
  3.2 1.2 copy-start.2
  4.4 0.7 copy-start.3
  175.2 88.7 %copy-start.4 = (s32[128,1]{0,1:T(1,128)S(1)}, s32[128,1]{0,1:T(1,128)}, u32[]{:S(2)}) copy-start(s32[128,1]{0,1:T(1,128)} %param.7) | copy-start | bytes 1540

commit v2 on v1

v2 whole, which is shorter than its diff:
```python
import jax
import jax.numpy as jnp
from jax import lax
from jax.experimental import pallas as pl
from jax.experimental.pallas import tpu as pltpu
from jax.sharding import PartitionSpec as P

HEADS = 32
HEAD = 128
TOK = 128
CLUSTERS = 128
MOST = 2
GROUPS = 4
SHARE = HEADS // GROUPS
UNIT = SHARE * MOST
DEVICES = CLUSTERS * GROUPS
ROWS = DEVICES * MOST
QBLK = 256
SOURCES = QBLK // MOST
CHUNK = 16
VMEM = 56 * 1024 * 1024
EMPTY = 256.0
MASKED = -1e30
FACTOR = 1.4426950408889634 / HEAD**0.5
BF16 = jnp.bfloat16
F32 = jnp.float32


def iota(shape, dim):
    return lax.broadcasted_iota(jnp.int32, shape, dim)


def spread_matrix(inverse):
    size = CHUNK * UNIT
    out, src = iota((size, size), 0), iota((size, size), 1)
    if inverse:
        out, src = src, out
    h, d, s = out // (CHUNK * MOST), (out // MOST) % CHUNK, out % MOST
    return (src == d * UNIT + h * MOST + s).astype(F32).astype(BF16)


def slot_onehot(row):
    row = row.astype(F32)
    above, across = iota((TOK, TOK), 0), iota((TOK, TOK), 1)
    col = jnp.sum(jnp.where(above == across, row, 0.0), axis=1, keepdims=True)
    earlier = (col == row) & (above < across)
    slots = row * MOST + jnp.sum(earlier.astype(F32), axis=0, keepdims=True)
    return (iota((CLUSTERS * MOST, TOK), 0).astype(F32) == slots).astype(F32)


def dot(a, b):
    return jnp.dot(a, b, preferred_element_type=F32)


def pack_kernel(row_ref, q_ref, k_ref, v_ref, out_ref):
    onehot = slot_onehot(row_ref[...])
    filled = jnp.sum(onehot, axis=1, keepdims=True) > 0.5
    onehot = onehot.astype(BF16)
    empty_entry = jnp.where(filled | (iota((1, HEAD), 1) > 0), 0.0, EMPTY)
    empty_entry = jnp.concatenate([empty_entry] * SHARE, axis=1)
    scatter = spread_matrix(True)
    rows = [dot(onehot, ref[...]) for ref in (q_ref, k_ref, v_ref)]
    rows[1] = rows[1] + empty_entry
    rows = [one.astype(BF16) for one in rows]
    width = CHUNK * MOST
    for block in range(CLUSTERS // CHUNK):
        tall = jnp.concatenate(
            [
                jnp.concatenate(
                    [
                        one[block * width : (block + 1) * width, h * HEAD : (h + 1) * HEAD]
                        for h in range(SHARE)
                    ],
                    axis=0,
                )
                for one in rows
            ],
            axis=1,
        )
        mixed = dot(scatter, tall).astype(BF16)
        for index in range(3):
            out_ref[
                block * CHUNK : (block + 1) * CHUNK, 0, index * UNIT : (index + 1) * UNIT, :
            ] = mixed[:, index * HEAD : (index + 1) * HEAD].reshape(CHUNK, UNIT, HEAD)


def pack(row, queries, keys, values):
    data = pl.BlockSpec((TOK, SHARE * HEAD), lambda g: (0, g))
    return pl.pallas_call(
        pack_kernel,
        grid=(GROUPS,),
        in_specs=[pl.BlockSpec((1, TOK), lambda g: (0, 0)), data, data, data],
        out_specs=pl.BlockSpec((CLUSTERS, 1, 3 * UNIT, HEAD), lambda g: (0, g, 0, 0)),
        out_shape=jax.ShapeDtypeStruct((CLUSTERS, GROUPS, 3 * UNIT, HEAD), BF16),
        compiler_params=pltpu.CompilerParams(vmem_limit_bytes=VMEM),
        name="pack",
    )(row, queries, keys, values)


def attend_kernel(in_ref, out_ref, k_scr, v_scr, q_scr, o_scr, mark_scr):
    step = pl.program_id(0)
    gather, scatter = spread_matrix(False), spread_matrix(True)
    first_lane = iota((QBLK, HEAD), 1) == 0

    def regroup(block):
        part = in_ref[block * CHUNK : (block + 1) * CHUNK, :, :]
        tall = jnp.concatenate(
            [
                part[:, i * UNIT : (i + 1) * UNIT, :].reshape(CHUNK * UNIT, HEAD)
                for i in range(3)
            ],
            axis=1,
        )
        mixed = dot(gather, tall).astype(BF16)
        width = CHUNK * MOST
        start = pl.multiple_of(step * QBLK + block * width, width)
        q_scr[:, block * width : (block + 1) * width, :] = mixed[:, :HEAD].reshape(
            SHARE, width, HEAD
        )
        k_scr[:, pl.ds(start, width), :] = mixed[:, HEAD : 2 * HEAD].reshape(SHARE, width, HEAD)
        v_scr[:, pl.ds(start, width), :] = mixed[:, 2 * HEAD :].reshape(SHARE, width, HEAD)

    for block in range(SOURCES // CHUNK):
        regroup(block)

    here = pl.multiple_of(step * QBLK, QBLK)
    empty = k_scr[0, pl.ds(here, QBLK), :].astype(F32) > EMPTY / 2
    mark_scr[pl.ds(here, QBLK), :] = jnp.where(empty & first_lane, MASKED, 0.0).astype(BF16)

    def queries_of(block):
        start, stop = block * QBLK, (block + 1) * QBLK
        unit = first_lane.astype(F32).astype(BF16)
        later = iota((QBLK, QBLK), 1) > iota((QBLK, QBLK), 0)
        ones = jnp.ones((stop, HEAD), BF16)
        for h in range(SHARE):
            q = jnp.concatenate([q_scr[h], unit], axis=1)
            k = jnp.concatenate([k_scr[h, 0:stop, :], mark_scr[0:stop, :]], axis=1)
            v = jnp.concatenate([v_scr[h, 0:stop, :], ones], axis=1)
            scores = lax.dot_general(
                q, k, (((1,), (1,)), ((), ())), preferred_element_type=F32
            )
            last = jnp.where(later, MASKED, scores[:, start:stop])
            if block:
                scores = jnp.concatenate([scores[:, :start], last], axis=1)
            else:
                scores = last
            top = jnp.max(scores, axis=1, keepdims=True)
            weights = jnp.exp2((scores - top) * FACTOR)
            mixed = dot(weights.astype(BF16), v)
            o_scr[h] = (mixed[:, :HEAD] / mixed[:, HEAD:]).astype(BF16)

    for block in range(ROWS // QBLK):
        pl.when(step == block)(lambda block=block: queries_of(block))

    for block in range(SOURCES // CHUNK):
        width = CHUNK * MOST
        tall = o_scr[:, block * width : (block + 1) * width, :].reshape(CHUNK * UNIT, HEAD)
        mixed = dot(scatter, tall).astype(BF16)
        out_ref[block * CHUNK : (block + 1) * CHUNK, :, :] = mixed.reshape(CHUNK, UNIT, HEAD)


def attend(received):
    held = pltpu.VMEM((SHARE, ROWS, HEAD), BF16)
    part = pltpu.VMEM((SHARE, QBLK, HEAD), BF16)
    return pl.pallas_call(
        attend_kernel,
        grid=(ROWS // QBLK,),
        in_specs=[pl.BlockSpec((SOURCES, 3 * UNIT, HEAD), lambda b: (b, 0, 0))],
        out_specs=pl.BlockSpec((SOURCES, UNIT, HEAD), lambda b: (b, 0, 0)),
        out_shape=jax.ShapeDtypeStruct((DEVICES, UNIT, HEAD), BF16),
        scratch_shapes=[held, held, part, part, pltpu.VMEM((ROWS, HEAD), BF16)],
        compiler_params=pltpu.CompilerParams(vmem_limit_bytes=VMEM),
        name="attend",
    )(received)


def unpack_kernel(row_ref, in_ref, out_ref):
    onehot = slot_onehot(row_ref[...]).astype(BF16)
    gather = spread_matrix(False)
    width = CHUNK * MOST
    blocks = []
    for block in range(CLUSTERS // CHUNK):
        tall = in_ref[block * CHUNK : (block + 1) * CHUNK, 0, :, :].reshape(CHUNK * UNIT, HEAD)
        mixed = dot(gather, tall).astype(BF16)
        blocks.append(
            jnp.concatenate([mixed[h * width : (h + 1) * width, :] for h in range(SHARE)], axis=1)
        )
    rows = jnp.concatenate(blocks, axis=0)
    out_ref[...] = lax.dot_general(
        onehot, rows, (((0,), (0,)), ((), ())), preferred_element_type=F32
    ).astype(BF16)


def unpack(row, back):
    return pl.pallas_call(
        unpack_kernel,
        grid=(GROUPS,),
        in_specs=[
            pl.BlockSpec((1, TOK), lambda g: (0, 0)),
            pl.BlockSpec((CLUSTERS, 1, UNIT, HEAD), lambda g: (0, g, 0, 0)),
        ],
        out_specs=pl.BlockSpec((TOK, SHARE * HEAD), lambda g: (0, g)),
        out_shape=jax.ShapeDtypeStruct((TOK, HEADS * HEAD), BF16),
        compiler_params=pltpu.CompilerParams(vmem_limit_bytes=VMEM),
        name="unpack",
    )(row, back)


def exchange(data):
    return lax.all_to_all(data, ("seq", "blk"), split_axis=0, concat_axis=0, tiled=True)


def body(queries, keys, values, cluster_ids):
    row = cluster_ids.reshape(1, TOK)
    sent = pack(row, queries, keys, values)
    received = exchange(sent.reshape(DEVICES, 3 * UNIT, HEAD))
    mixed = attend(received)
    back = exchange(mixed)
    return unpack(row, back.reshape(CLUSTERS, GROUPS, UNIT, HEAD))


def solution(mesh):
    spec = P(("seq", "blk"), None)
    return jax.shard_map(
        body, mesh=mesh, in_specs=(spec,) * 4, out_specs=spec, check_vma=False
    )
```

time: 267 us -> 258 us (0.966)
  Pallas kernels: 32.5 us -> 27.4 us
  local copies, waits for them, and re-layouts: 5.09 us -> 0 us
    pallas_call x3, Pallas kernels: 32.5 us -> 27.4 us  [the longest x1 14.6 us: attend(): pl.pallas_call(attend_kernel, grid=(ROWS // QBLK,), in_specs=[pl.BlockSpe...]
    unnamed x11 -> x0, local copies, waits for them, and re-layouts: 5.09 us -> none
where the time goes in v2:
time: 258 us; the launch traced here: 257 us
  blocking collectives  230 us (89%)
  Pallas kernels  27.4 us (11%)
    all_to_all x2, blocking collectives, exchange(): lax.all_to_all(data, ('seq', 'blk'), split_axis=0, concat_axis=0, tiled=T...  230 us
    pallas_call x1, Pallas kernels, attend(): pl.pallas_call(attend_kernel, grid=(ROWS // QBLK,), in_specs=[pl.BlockSpe...  14.6 us
    pallas_call x1, Pallas kernels, pack(): pl.pallas_call(pack_kernel, grid=(GROUPS,), in_specs=[pl.BlockSpec((1, TO...  7.98 us

profile of v2, /device:TPU:1, one launch (start us, length us, event | category | flops | bytes accessed | tf_op | source)
XLA Modules:
  0.0 257.3 jit_solution(17217034942876189827)
XLA Ops:
  0.0 8.0 %pack.1 = bf16[128,4,48,128]{3,2,1,0:T(8,128)(2,1)} custom-call(s32[1,128]{1,0:T(1,128)} %bitcast.5, bf16[128,4096]{1,0:T(8,128)(2,1)} %q_ref.1, bf16[128,4096]{1,0:T(8,128)(2,1)} %k_ref.1, bf16[128,4096]{1,0:T(8,128)(2,1)} %v_ref.1), custom_call_target="tpu_custom_call" | custom-call | tf_op jit(solution)/shard_map/pack/pallas_call | solution.py:89
  8.0 164.4 %all_to_all.10.in_ref = bf16[512,48,128]{2,1,0:T(8,128)(2,1)} all-to-all(bf16[512,48,128]{2,1,0:T(8,128)(2,1)} %bitcast.3), channel_id=1, replica_groups=mesh['seq'=128,'blk'=4] {'seq','blk'}, dimensions={0} | all-to-all | bytes 12582912 | tf_op jit(solution)/shard_map/all_to_all | solution.py:210
  172.4 14.6 %attend.1 = bf16[512,16,128]{2,1,0:T(8,128)(2,1)} custom-call(bf16[512,48,128]{2,1,0:T(8,128)(2,1)} %all_to_all.10.in_ref), custom_call_target="tpu_custom_call" | custom-call | tf_op jit(solution)/shard_map/attend/pallas_call | solution.py:165
  187.1 65.5 %all_to_all.11 = bf16[512,16,128]{2,1,0:T(8,128)(2,1)} all-to-all(bf16[512,16,128]{2,1,0:T(8,128)(2,1)} %attend.1), channel_id=1, replica_groups=mesh['seq'=128,'blk'=4] {'seq','blk'}, dimensions={0} | all-to-all | bytes 4194304 | tf_op jit(solution)/shard_map/all_to_all | solution.py:210
  252.5 4.7 %unpack.1 = bf16[128,4096]{1,0:T(8,128)(2,1)} custom-call(s32[1,128]{1,0:T(1,128)} %bitcast.6, bf16[128,4,16,128]{3,2,1,0:T(8,128)(2,1)} %bitcast.4), custom_call_target="tpu_custom_call" | custom-call | tf_op jit(solution)/shard_map/unpack/pallas_call | solution.py:195

commit v3 on v2

--- a/solution.py
+++ b/solution.py
@@ -19,6 +19,10 @@
 SOURCES = QBLK // MOST
 CHUNK = 16
 VMEM = 56 * 1024 * 1024
+EXTRA = 5
+TAIL = 16
+MESSAGE = 3 * SHARE + TAIL
+NONE = -64.0
 EMPTY = 256.0
 MASKED = -1e30
 FACTOR = 1.4426950408889634 / HEAD**0.5
@@ -206,17 +210,230 @@
     )(row, back)
 
 
+def token_ranks(row):
+    row = row.astype(F32)
+    above, across = iota((TOK, TOK), 0), iota((TOK, TOK), 1)
+    col = jnp.sum(jnp.where(above == across, row, 0.0), axis=1, keepdims=True)
+    same = col == row
+    second = jnp.sum((same & (above < across)).astype(F32), axis=0, keepdims=True)
+    second_col = jnp.sum((same & (across < above)).astype(F32), axis=1, keepdims=True)
+    group, group_col = jnp.floor(row / SHARE), jnp.floor(col / SHARE)
+    lower = (second_col > 0.5) & (group_col == group) & (col < row)
+    rank = jnp.sum(lower.astype(F32), axis=0, keepdims=True)
+    return row, group, second, rank
+
+
+def bits(mask):
+    return mask.astype(F32).astype(BF16)
+
+
+def lean_pack_kernel(row_ref, q_ref, k_ref, v_ref, out_ref):
+    row, group, second, rank = token_ranks(row_ref[...])
+    is_second = second > 0.5
+    mine = iota((CLUSTERS, TOK), 0).astype(F32) == row
+    first = mine & jnp.logical_not(is_second)
+    filled = jnp.sum(first.astype(F32), axis=1, keepdims=True) > 0.5
+    empty_entry = jnp.where(filled | (iota((1, HEAD), 1) > 0), 0.0, EMPTY)
+
+    seconds = (mine & is_second).astype(F32)
+    there = jnp.sum(seconds, axis=1, keepdims=True) > 0.5
+    code = jnp.where(there, jnp.sum(seconds * rank, axis=1, keepdims=True), NONE)
+    short = jnp.max(second * (rank + 1.0), axis=1, keepdims=True) > EXTRA + 0.5
+    place, lane = iota((CLUSTERS, HEAD), 0) % SHARE, iota((CLUSTERS, HEAD), 1)
+    codes = jnp.where(lane == place, code, 0.0)
+    codes = jnp.where((lane == SHARE) & short, 1.0, codes).astype(BF16)
+    size = CLUSTERS // SHARE * TAIL
+    number = iota((size, CLUSTERS), 0)
+    last = (number % TAIL == TAIL - 1) & (number // TAIL == iota((size, CLUSTERS), 1) // SHARE)
+    notes = dot(bits(last), codes)
+
+    fits = is_second & (rank < EXTRA - 0.5)
+    slot = jnp.where(fits, group * TAIL + rank, -1000.0)
+    number = number.astype(F32)
+    chosen = jnp.concatenate([bits(number == slot + EXTRA * i) for i in range(3)], axis=1)
+    data = [ref[...] for ref in (q_ref, k_ref, v_ref)]
+    tail = dot(chosen, jnp.concatenate(data, axis=0))
+    tail = tail + jnp.concatenate([notes] * SHARE, axis=1)
+    q, k, v = [dot(bits(first), one) for one in data]
+    k = k + jnp.concatenate([empty_entry] * SHARE, axis=1)
+    for j in range(CLUSTERS // SHARE):
+        rows = slice(j * SHARE, (j + 1) * SHARE)
+        message = jnp.concatenate(
+            [q[rows], k[rows], tail[j * TAIL : (j + 1) * TAIL], v[rows]], axis=0
+        ).astype(BF16)
+        for h in range(SHARE):
+            out_ref[j, h] = message[:, h * HEAD : (h + 1) * HEAD]
+
+
+def lean_pack(row, queries, keys, values):
+    data = pl.BlockSpec((TOK, SHARE * HEAD), lambda g: (0, g))
+    groups = CLUSTERS // SHARE
+    return pl.pallas_call(
+        lean_pack_kernel,
+        grid=(GROUPS,),
+        in_specs=[pl.BlockSpec((1, TOK), lambda g: (0, 0)), data, data, data],
+        out_specs=pl.BlockSpec((groups, SHARE, MESSAGE, HEAD), lambda g: (0, g, 0, 0)),
+        out_shape=jax.ShapeDtypeStruct((groups, HEADS, MESSAGE, HEAD), BF16),
+        compiler_params=pltpu.CompilerParams(vmem_limit_bytes=VMEM),
+        name="lean_pack",
+    )(row, queries, keys, values)
+
+
+def lean_attend_kernel(in_ref, out_ref, k_scr, v_scr, q_scr, o_scr, code_scr):
+    step = pl.program_id(0)
+    here = pl.multiple_of(step * QBLK, QBLK)
+    size = SHARE * CHUNK
+    row, col = iota((size, size), 0), iota((size, size), 1)
+    turn = bits(col == row % CHUNK * SHARE + row // CHUNK)
+    turn_back = bits(row == col % CHUNK * SHARE + col // CHUNK)
+    lane = iota((size, HEAD), 1)
+    own_lane = lane == iota((size, HEAD), 0) // CHUNK
+    wide_row, wide_col = iota((size, CHUNK * TAIL), 0), iota((size, CHUNK * TAIL), 1)
+    own_tail = wide_row % CHUNK == wide_col // TAIL
+    pick_notes = bits(own_tail & (wide_col % TAIL == TAIL - 1))
+    tail_place = jnp.where(own_tail, (wide_col % TAIL).astype(F32), -200.0)
+    back_place = jnp.where(row % CHUNK == col // SHARE, (col % SHARE).astype(F32), -200.0)
+
+    def keep(part, start, q, k, v):
+        shape = (SHARE, CHUNK, HEAD)
+        q_scr[:, part : part + CHUNK, :] = q.astype(BF16).reshape(shape)
+        v_scr[:, pl.ds(start, CHUNK), :] = v.astype(BF16).reshape(shape)
+        k_scr[:, pl.ds(start, CHUNK), :HEAD] = k.astype(BF16).reshape(shape)
+        mark = jnp.where(k > EMPTY / 2, MASKED, 0.0)
+        k_scr[:, pl.ds(start, CHUNK), HEAD:] = mark.astype(BF16).reshape(shape)
+
+    for block in range(SOURCES // CHUNK):
+        part = in_ref[block * CHUNK : (block + 1) * CHUNK, :, :].astype(F32)
+        at = 2 * SHARE
+        pieces = [part[:, :SHARE], part[:, SHARE:at], part[:, at + TAIL :]]
+        tall = jnp.concatenate([one.reshape(size, HEAD) for one in pieces], axis=1)
+        mixed = dot(turn, tall.astype(BF16))
+        start = pl.multiple_of(here + block * CHUNK, CHUNK)
+        keep(block * CHUNK, start, mixed[:, :HEAD], mixed[:, HEAD : 2 * HEAD], mixed[:, 2 * HEAD :])
+
+        tail = part[:, at : at + TAIL].reshape(CHUNK * TAIL, HEAD).astype(BF16)
+        notes = dot(pick_notes, tail)
+        code = jnp.sum(jnp.where(own_lane, notes, 0.0), axis=1, keepdims=True)
+        code_scr[block] = jnp.broadcast_to(code, (size, HEAD))
+        chosen = jnp.concatenate([bits(tail_place == code + EXTRA * i) for i in range(3)], axis=0)
+        found = dot(chosen, tail)
+        k = found[size : 2 * size] + jnp.where((code < NONE / 2) & (lane == 0), EMPTY, 0.0)
+        start = pl.multiple_of(here + SOURCES + block * CHUNK, CHUNK)
+        keep(SOURCES + block * CHUNK, start, found[:size], k, found[2 * size :])
+
+    def queries_of(block):
+        start, stop = block * QBLK, (block + 1) * QBLK
+        unit = bits(iota((QBLK, HEAD), 1) == 0)
+        row, col = iota((QBLK, QBLK), 0), iota((QBLK, QBLK), 1)
+        later = col % SOURCES * MOST + col // SOURCES > row % SOURCES * MOST + row // SOURCES
+        ones = jnp.ones((stop, HEAD), BF16)
+        for c in range(SHARE):
+            q = jnp.concatenate([q_scr[c], unit], axis=1)
+            v = jnp.concatenate([v_scr[c, 0:stop, :], ones], axis=1)
+            scores = lax.dot_general(
+                q, k_scr[c, 0:stop, :], (((1,), (1,)), ((), ())), preferred_element_type=F32
+            )
+            last = jnp.where(later, MASKED, scores[:, start:stop])
+            if block:
+                scores = jnp.concatenate([scores[:, :start], last], axis=1)
+            else:
+                scores = last
+            top = jnp.max(scores, axis=1, keepdims=True)
+            weights = jnp.exp2((scores - top) * FACTOR)
+            mixed = dot(weights.astype(BF16), v)
+            o_scr[c] = (mixed[:, :HEAD] / mixed[:, HEAD:]).astype(BF16)
+
+    for block in range(ROWS // QBLK):
+        pl.when(step == block)(lambda block=block: queries_of(block))
+
+    for block in range(SOURCES // CHUNK):
+        begin = block * CHUNK
+        shape = (CHUNK, SHARE, HEAD)
+        firsts = dot(turn_back, o_scr[:, begin : begin + CHUNK, :].reshape(size, HEAD))
+        begin = begin + SOURCES
+        chosen = bits(back_place == code_scr[block])
+        seconds = lax.dot_general(
+            chosen,
+            o_scr[:, begin : begin + CHUNK, :].reshape(size, HEAD),
+            (((0,), (0,)), ((), ())),
+            preferred_element_type=F32,
+        )
+        both = jnp.concatenate([firsts.reshape(shape), seconds.reshape(shape)], axis=1)
+        out_ref[block * CHUNK : (block + 1) * CHUNK, :, :] = both.astype(BF16)
+
+
+def lean_attend(received):
+    part = pltpu.VMEM((SHARE, QBLK, HEAD), BF16)
+    return pl.pallas_call(
+        lean_attend_kernel,
+        grid=(ROWS // QBLK,),
+        in_specs=[pl.BlockSpec((SOURCES, MESSAGE, HEAD), lambda b: (b, 0, 0))],
+        out_specs=pl.BlockSpec((SOURCES, UNIT, HEAD), lambda b: (b, 0, 0)),
+        out_shape=jax.ShapeDtypeStruct((DEVICES, UNIT, HEAD), BF16),
+        scratch_shapes=[
+            pltpu.VMEM((SHARE, ROWS, 2 * HEAD), BF16),
+            pltpu.VMEM((SHARE, ROWS, HEAD), BF16),
+            part,
+            part,
+            pltpu.VMEM((SOURCES // CHUNK, SHARE * CHUNK, HEAD), F32),
+        ],
+        compiler_params=pltpu.CompilerParams(vmem_limit_bytes=VMEM),
+        name="lean_attend",
+    )(received)
+
+
+def lean_unpack_kernel(row_ref, in_ref, out_ref):
+    row, group, second, rank = token_ranks(row_ref[...])
+    slot = group * UNIT + jnp.where(second > 0.5, SHARE + rank, row - group * SHARE)
+    onehot = bits(iota((CLUSTERS // SHARE * UNIT, TOK), 0).astype(F32) == slot)
+    rows = jnp.concatenate(
+        [
+            jnp.concatenate([in_ref[j, h] for h in range(SHARE)], axis=1)
+            for j in range(CLUSTERS // SHARE)
+        ],
+        axis=0,
+    )
+    out_ref[...] = lax.dot_general(
+        onehot, rows, (((0,), (0,)), ((), ())), preferred_element_type=F32
+    ).astype(BF16)
+
+
+def lean_unpack(row, back):
+    groups = CLUSTERS // SHARE
+    return pl.pallas_call(
+        lean_unpack_kernel,
+        grid=(GROUPS,),
+        in_specs=[
+            pl.BlockSpec((1, TOK), lambda g: (0, 0)),
+            pl.BlockSpec((groups, SHARE, UNIT, HEAD), lambda g: (0, g, 0, 0)),
+        ],
+        out_specs=pl.BlockSpec((TOK, SHARE * HEAD), lambda g: (0, g)),
+        out_shape=jax.ShapeDtypeStruct((TOK, HEADS * HEAD), BF16),
+        compiler_params=pltpu.CompilerParams(vmem_limit_bytes=VMEM),
+        name="lean_unpack",
+    )(row, back)
+
+
 def exchange(data):
     return lax.all_to_all(data, ("seq", "blk"), split_axis=0, concat_axis=0, tiled=True)
 
 
 def body(queries, keys, values, cluster_ids):
     row = cluster_ids.reshape(1, TOK)
-    sent = pack(row, queries, keys, values)
-    received = exchange(sent.reshape(DEVICES, 3 * UNIT, HEAD))
-    mixed = attend(received)
-    back = exchange(mixed)
-    return unpack(row, back.reshape(CLUSTERS, GROUPS, UNIT, HEAD))
+    sent = lean_pack(row, queries, keys, values)
+    received = exchange(sent.reshape(DEVICES, MESSAGE, HEAD))
+    short = jnp.max(received[:, 2 * SHARE + TAIL - 1, SHARE]) > 0
+
+    def lean(received, row, queries, keys, values):
+        back = exchange(lean_attend(received))
+        return lean_unpack(row, back.reshape(CLUSTERS // SHARE, HEADS, UNIT, HEAD))
+
+    def full(received, row, queries, keys, values):
+        sent = pack(row, queries, keys, values)
+        back = exchange(attend(exchange(sent.reshape(DEVICES, 3 * UNIT, HEAD))))
+        return unpack(row, back.reshape(CLUSTERS, GROUPS, UNIT, HEAD))
+
+    return lax.cond(short, full, lean, received, row, queries, keys, values)
 
 
 def solution(mesh):

time: 258 us -> 242 us (0.938)
  blocking collectives: 230 us -> 65.1 us
  waiting for transfers between devices: 0 us -> 118 us
  starting transfers between devices: 0 us -> 24 us
    all_to_all x2 -> x1, blocking collectives: 230 us -> 65.1 us  [exchange(): lax.all_to_all(data, ('seq', 'blk'), split_axis=0, concat_axis=0, tiled=T...]
    all_to_all x0 -> x1, waiting for transfers between devices: none -> 118 us  [exchange(): lax.all_to_all(data, ('seq', 'blk'), split_axis=0, concat_axis=0, tiled=T...]
    all_to_all x0 -> x1, starting transfers between devices: none -> 24 us  [exchange(): lax.all_to_all(data, ('seq', 'blk'), split_axis=0, concat_axis=0, tiled=T...]
  transfers between devices with their start and end apart: 0 -> 1, of which waited for: 0 -> 1; matrix products, arithmetic and copies ran while one was open for 0% -> 0% of each run, Pallas kernels for 0% -> 0%
where the time goes in v3:
time: 242 us
  waiting for transfers between devices  118 us (49%)
  blocking collectives  65.1 us (27%)
  Pallas kernels  29.3 us (12%)
  starting transfers between devices  24 us (10%)
  other arithmetic  2.44 us (1%)
    all_to_all x1, waiting for transfers between devices, exchange(): lax.all_to_all(data, ('seq', 'blk'), split_axis=0, concat_axis=0, tiled=T...  118 us
    all_to_all x1, blocking collectives, exchange(): lax.all_to_all(data, ('seq', 'blk'), split_axis=0, concat_axis=0, tiled=T...  65.1 us
    all_to_all x1, starting transfers between devices, exchange(): lax.all_to_all(data, ('seq', 'blk'), split_axis=0, concat_axis=0, tiled=T...  24 us
    pallas_call x1, Pallas kernels, lean_attend(): pl.pallas_call(lean_attend_kernel, grid=(ROWS // QBLK,), in_specs=[pl.Blo...  19.2 us
    pallas_call x1, Pallas kernels, lean_pack(): pl.pallas_call(lean_pack_kernel, grid=(GROUPS,), in_specs=[pl.BlockSpec((...  6.6 us
  transfers between devices with their start and end apart: 1, of which 1 were waited for; matrix products, arithmetic and copies ran while one was open for 0% of the time, Pallas kernels for 0%

profile of v3, /device:TPU:1, one launch (start us, length us, event | category | flops | bytes accessed | tf_op | source)
XLA Modules:
  0.0 241.6 jit_solution(9861460122462628740)
XLA Ops:
  0.0 6.6 %lean_pack.1 = bf16[16,32,40,128]{3,2,1,0:T(8,128)(2,1)} custom-call(s32[1,128]{1,0:T(1,128)} %bitcast.9, bf16[128,4096]{1,0:T(8,128)(2,1)} %q_ref.1, bf16[128,4096]{1,0:T(8,128)(2,1)} %k_ref.1, bf16[128,4096]{1,0:T(8,128)(2,1)} %v_ref.1), custom_call_target="tpu_custom_call" | custom-call | tf_op jit(solution)/shard_map/lean_pack/pallas_call | solution.py:271
  6.6 0.0 copy-start
  6.6 0.0 copy-start.1
  6.6 0.0 copy-start.2
  6.6 0.0 copy-start.4
  6.6 24.0 %all-to-all-start.3 = ((bf16[512,40,128]{2,1,0:T(8,128)(2,1)}), bf16[512,40,128]{2,1,0:T(8,128)(2,1)}, u32[]{:S(2)}, u32[]{:S(2)}) async-start(bf16[512,40,128]{2,1,0:T(8,128)(2,1)} %bitcast.6), calls=%async_computation.3 | async-start | bytes 10485760 | tf_op jit(solution)/shard_map/all_to_all | solution.py:418
  30.6 118.4 %all-to-all-done.3 = bf16[512,40,128]{2,1,0:T(8,128)(2,1)} async-done(((bf16[512,40,128]{2,1,0:T(8,128)(2,1)}), bf16[512,40,128]{2,1,0:T(8,128)(2,1)}, u32[]{:S(2)}, u32[]{:S(2)}) %all-to-all-start.3) | async-done | bytes 5242912 | tf_op jit(solution)/shard_map/all_to_all | solution.py:418
  149.0 2.4 %slice_reduce_fusion = bf16[]{:T(256)} fusion(bf16[512,40,128]{2,1,0:T(8,128)(2,1)} %all-to-all-done.3), kind=kLoop, calls=%fused_computation | loop fusion | flops 511 | bytes 1026 | tf_op jit(solution)/shard_map/reduce_max | solution.py:425
  152.1 0.0 copy-done
  152.1 0.0 copy-done.1
  152.1 0.0 copy-done.2
  152.1 0.0 copy-done.4
  152.1 88.5 %conditional.1 = (bf16[128,4096]{1,0:T(8,128)(2,1)S(1)}) conditional(s32[]{:T(128)} %convert_element_type.3, (bf16[512,40,128]{2,1,0:T(8,128)(2,1)}, s32[1,128]{1,0:T(1,128)S(1)}) %tuple.21, (s32[1,128]{1,0:T(1,128)S(1)}, bf16[128,4096]{1,0:T(8,128)(2,1)S(1)}, bf16[128,4096]{1,0:T(8,128)(2,1)S(1)}, bf16[128,4096]{1,0:T(8,128)(2,1)S(1)}) %tuple.22), branch_computations={%region_1.0_spmd, %region_2.0_spmd} | conditional | bytes 16777224 | solution.py:436
  152.3 19.2 %lean_attend.1 = bf16[512,16,128]{2,1,0:T(8,128)(2,1)} custom-call(bf16[512,40,128]{2,1,0:T(8,128)(2,1)} %get-tuple-element.21.in_ref), custom_call_target="tpu_custom_call" | custom-call | tf_op jit(solution)/shard_map/cond/branch_0_fun/lean_attend/pallas_call | solution.py:367
  171.5 65.1 %all_to_all.17 = bf16[512,16,128]{2,1,0:T(8,128)(2,1)} all-to-all(bf16[512,16,128]{2,1,0:T(8,128)(2,1)} %lean_attend.1), channel_id=1, replica_groups=mesh['seq'=128,'blk'=4] {'seq','blk'}, dimensions={0} | all-to-all | bytes 4194304 | tf_op jit(solution)/shard_map/cond/branch_0_fun/all_to_all | solution.py:418
  236.5 3.5 %lean_unpack.1 = bf16[128,4096]{1,0:T(8,128)(2,1)S(1)} custom-call(s32[1,128]{1,0:T(1,128)S(1)} %get-tuple-element.20.row_ref, bf16[16,32,16,128]{3,2,1,0:T(8,128)(2,1)} %bitcast.7), custom_call_target="tpu_custom_call" | custom-call | tf_op jit(solution)/shard_map/cond/branch_0_fun/lean_unpack/pallas_call | solution.py:403
  240.6 0.0 copy-start.3
  240.6 1.0 copy-done.3
Async XLA Ops:
  6.6 145.5 %copy-start = (bf16[128,4096]{1,0:T(8,128)(2,1)S(1)}, bf16[128,4096]{1,0:T(8,128)(2,1)}, u32[]{:S(2)}) copy-start(bf16[128,4096]{1,0:T(8,128)(2,1)} %q_ref.1) | copy-start | bytes 3145732
  6.6 145.5 %copy-start.1 = (bf16[128,4096]{1,0:T(8,128)(2,1)S(1)}, bf16[128,4096]{1,0:T(8,128)(2,1)}, u32[]{:S(2)}) copy-start(bf16[128,4096]{1,0:T(8,128)(2,1)} %k_ref.1) | copy-start | bytes 3145732
  6.6 145.5 %copy-start.2 = (bf16[128,4096]{1,0:T(8,128)(2,1)S(1)}, bf16[128,4096]{1,0:T(8,128)(2,1)}, u32[]{:S(2)}) copy-start(bf16[128,4096]{1,0:T(8,128)(2,1)} %v_ref.1) | copy-start | bytes 3145732
  6.6 145.5 %copy-start.4 = (s32[128,1]{0,1:T(1,128)S(1)}, s32[128,1]{0,1:T(1,128)}, u32[]{:S(2)}) copy-start(s32[128,1]{0,1:T(1,128)} %param.9) | copy-start | bytes 1540
  6.6 142.4 %all-to-all-start.3 = ((bf16[512,40,128]{2,1,0:T(8,128)(2,1)}), bf16[512,40,128]{2,1,0:T(8,128)(2,1)}, u32[]{:S(2)}, u32[]{:S(2)}) async-start(bf16[512,40,128]{2,1,0:T(8,128)(2,1)} %bitcast.6), calls=%async_computation.3 | async-start | bytes 10485760 | tf_op jit(solution)/shard_map/all_to_all | solution.py:418
  240.6 1.0 copy-start.3

commit v4 on v3

--- a/solution.py
+++ b/solution.py
@@ -227,35 +227,43 @@
     return mask.astype(F32).astype(BF16)
 
 
-def lean_pack_kernel(row_ref, q_ref, k_ref, v_ref, out_ref):
-    row, group, second, rank = token_ranks(row_ref[...])
-    is_second = second > 0.5
-    mine = iota((CLUSTERS, TOK), 0).astype(F32) == row
-    first = mine & jnp.logical_not(is_second)
-    filled = jnp.sum(first.astype(F32), axis=1, keepdims=True) > 0.5
-    empty_entry = jnp.where(filled | (iota((1, HEAD), 1) > 0), 0.0, EMPTY)
-
-    seconds = (mine & is_second).astype(F32)
-    there = jnp.sum(seconds, axis=1, keepdims=True) > 0.5
-    code = jnp.where(there, jnp.sum(seconds * rank, axis=1, keepdims=True), NONE)
-    short = jnp.max(second * (rank + 1.0), axis=1, keepdims=True) > EXTRA + 0.5
-    place, lane = iota((CLUSTERS, HEAD), 0) % SHARE, iota((CLUSTERS, HEAD), 1)
-    codes = jnp.where(lane == place, code, 0.0)
-    codes = jnp.where((lane == SHARE) & short, 1.0, codes).astype(BF16)
-    size = CLUSTERS // SHARE * TAIL
-    number = iota((size, CLUSTERS), 0)
-    last = (number % TAIL == TAIL - 1) & (number // TAIL == iota((size, CLUSTERS), 1) // SHARE)
-    notes = dot(bits(last), codes)
-
-    fits = is_second & (rank < EXTRA - 0.5)
-    slot = jnp.where(fits, group * TAIL + rank, -1000.0)
-    number = number.astype(F32)
-    chosen = jnp.concatenate([bits(number == slot + EXTRA * i) for i in range(3)], axis=1)
+def lean_pack_kernel(
+    row_ref, q_ref, k_ref, v_ref, out_ref, first_scr, empty_scr, notes_scr, chosen_scr
+):
+    @pl.when(pl.program_id(0) == 0)
+    def prepare():
+        row, group, second, rank = token_ranks(row_ref[...])
+        is_second = second > 0.5
+        mine = iota((CLUSTERS, TOK), 0).astype(F32) == row
+        first = mine & jnp.logical_not(is_second)
+        first_scr[...] = bits(first)
+        filled = jnp.sum(first.astype(F32), axis=1, keepdims=True) > 0.5
+        empty_scr[...] = jnp.where(filled | (iota((1, HEAD), 1) > 0), 0.0, EMPTY)
+
+        seconds = (mine & is_second).astype(F32)
+        there = jnp.sum(seconds, axis=1, keepdims=True) > 0.5
+        code = jnp.where(there, jnp.sum(seconds * rank, axis=1, keepdims=True), NONE)
+        short = jnp.max(second * (rank + 1.0), axis=1, keepdims=True) > EXTRA + 0.5
+        place, lane = iota((CLUSTERS, HEAD), 0) % SHARE, iota((CLUSTERS, HEAD), 1)
+        codes = jnp.where(lane == place, code, 0.0)
+        codes = jnp.where((lane == SHARE) & short, 1.0, codes).astype(BF16)
+        size = CLUSTERS // SHARE * TAIL
+        number = iota((size, CLUSTERS), 0)
+        last = (number % TAIL == TAIL - 1) & (number // TAIL == iota((size, CLUSTERS), 1) // SHARE)
+        notes_scr[...] = dot(bits(last), codes)
+
+        fits = is_second & (rank < EXTRA - 0.5)
+        slot = jnp.where(fits, group * TAIL + rank, -1000.0)
+        number = number.astype(F32)
+        chosen_scr[...] = jnp.concatenate(
+            [bits(number == slot + EXTRA * i) for i in range(3)], axis=1
+        )
+
     data = [ref[...] for ref in (q_ref, k_ref, v_ref)]
-    tail = dot(chosen, jnp.concatenate(data, axis=0))
-    tail = tail + jnp.concatenate([notes] * SHARE, axis=1)
-    q, k, v = [dot(bits(first), one) for one in data]
-    k = k + jnp.concatenate([empty_entry] * SHARE, axis=1)
+    tail = dot(chosen_scr[...], jnp.concatenate(data, axis=0))
+    tail = tail + jnp.concatenate([notes_scr[...]] * SHARE, axis=1)
+    q, k, v = [dot(first_scr[...], one) for one in data]
+    k = k + jnp.concatenate([empty_scr[...]] * SHARE, axis=1)
     for j in range(CLUSTERS // SHARE):
         rows = slice(j * SHARE, (j + 1) * SHARE)
         message = jnp.concatenate(
@@ -274,14 +282,19 @@
         in_specs=[pl.BlockSpec((1, TOK), lambda g: (0, 0)), data, data, data],
         out_specs=pl.BlockSpec((groups, SHARE, MESSAGE, HEAD), lambda g: (0, g, 0, 0)),
         out_shape=jax.ShapeDtypeStruct((groups, HEADS, MESSAGE, HEAD), BF16),
+        scratch_shapes=[
+            pltpu.VMEM((CLUSTERS, TOK), BF16),
+            pltpu.VMEM((CLUSTERS, HEAD), F32),
+            pltpu.VMEM((groups * TAIL, HEAD), F32),
+            pltpu.VMEM((groups * TAIL, 3 * TOK), BF16),
+        ],
         compiler_params=pltpu.CompilerParams(vmem_limit_bytes=VMEM),
         name="lean_pack",
     )(row, queries, keys, values)
 
 
-def lean_attend_kernel(in_ref, out_ref, k_scr, v_scr, q_scr, o_scr, code_scr):
+def lean_attend_kernel(in_ref, out_ref, flag_ref, k_scr, v_scr, q_scr, o_scr, code_scr):
     step = pl.program_id(0)
-    here = pl.multiple_of(step * QBLK, QBLK)
     size = SHARE * CHUNK
     row, col = iota((size, size), 0), iota((size, size), 1)
     turn = bits(col == row % CHUNK * SHARE + row // CHUNK)
@@ -297,35 +310,44 @@
     def keep(part, start, q, k, v):
         shape = (SHARE, CHUNK, HEAD)
         q_scr[:, part : part + CHUNK, :] = q.astype(BF16).reshape(shape)
-        v_scr[:, pl.ds(start, CHUNK), :] = v.astype(BF16).reshape(shape)
-        k_scr[:, pl.ds(start, CHUNK), :HEAD] = k.astype(BF16).reshape(shape)
+        v_scr[:, start : start + CHUNK, :] = v.astype(BF16).reshape(shape)
+        k_scr[:, start : start + CHUNK, :HEAD] = k.astype(BF16).reshape(shape)
         mark = jnp.where(k > EMPTY / 2, MASKED, 0.0)
-        k_scr[:, pl.ds(start, CHUNK), HEAD:] = mark.astype(BF16).reshape(shape)
-
-    for block in range(SOURCES // CHUNK):
-        part = in_ref[block * CHUNK : (block + 1) * CHUNK, :, :].astype(F32)
-        at = 2 * SHARE
-        pieces = [part[:, :SHARE], part[:, SHARE:at], part[:, at + TAIL :]]
-        tall = jnp.concatenate([one.reshape(size, HEAD) for one in pieces], axis=1)
-        mixed = dot(turn, tall.astype(BF16))
-        start = pl.multiple_of(here + block * CHUNK, CHUNK)
-        keep(block * CHUNK, start, mixed[:, :HEAD], mixed[:, HEAD : 2 * HEAD], mixed[:, 2 * HEAD :])
-
-        tail = part[:, at : at + TAIL].reshape(CHUNK * TAIL, HEAD).astype(BF16)
-        notes = dot(pick_notes, tail)
-        code = jnp.sum(jnp.where(own_lane, notes, 0.0), axis=1, keepdims=True)
-        code_scr[block] = jnp.broadcast_to(code, (size, HEAD))
-        chosen = jnp.concatenate([bits(tail_place == code + EXTRA * i) for i in range(3)], axis=0)
-        found = dot(chosen, tail)
-        k = found[size : 2 * size] + jnp.where((code < NONE / 2) & (lane == 0), EMPTY, 0.0)
-        start = pl.multiple_of(here + SOURCES + block * CHUNK, CHUNK)
-        keep(SOURCES + block * CHUNK, start, found[:size], k, found[2 * size :])
+        k_scr[:, start : start + CHUNK, HEAD:] = mark.astype(BF16).reshape(shape)
+
+    def load_all(here):
+        flags = jnp.zeros((size, HEAD), F32)
+        for block in range(SOURCES // CHUNK):
+            part = in_ref[block * CHUNK : (block + 1) * CHUNK, :, :].astype(F32)
+            at = 2 * SHARE
+            pieces = [part[:, :SHARE], part[:, SHARE:at], part[:, at + TAIL :]]
+            tall = jnp.concatenate([one.reshape(size, HEAD) for one in pieces], axis=1)
+            mixed = dot(turn, tall.astype(BF16))
+            start = here + block * CHUNK
+            keep(block * CHUNK, start, mixed[:, :HEAD], mixed[:, HEAD : 2 * HEAD], mixed[:, 2 * HEAD :])
+
+            tail = part[:, at : at + TAIL].reshape(CHUNK * TAIL, HEAD).astype(BF16)
+            notes = dot(pick_notes, tail)
+            flags = jnp.maximum(flags, notes)
+            code = jnp.sum(jnp.where(own_lane, notes, 0.0), axis=1, keepdims=True)
+            code_scr[block] = jnp.broadcast_to(code, (size, HEAD))
+            chosen = jnp.concatenate([bits(tail_place == code + EXTRA * i) for i in range(3)], axis=0)
+            found = dot(chosen, tail)
+            k = found[size : 2 * size] + jnp.where((code < NONE / 2) & (lane == 0), EMPTY, 0.0)
+            start = here + SOURCES + block * CHUNK
+            keep(SOURCES + block * CHUNK, start, found[:size], k, found[2 * size :])
+
+        flags = jnp.max(flags, axis=0, keepdims=True)
+        if here:
+            flags = jnp.maximum(flags, flag_ref[0:1, :])
+        flag_ref[...] = jnp.broadcast_to(flags, flag_ref.shape)
 
     def queries_of(block):
         start, stop = block * QBLK, (block + 1) * QBLK
         unit = bits(iota((QBLK, HEAD), 1) == 0)
-        row, col = iota((QBLK, QBLK), 0), iota((QBLK, QBLK), 1)
-        later = col % SOURCES * MOST + col // SOURCES > row % SOURCES * MOST + row // SOURCES
+        row, col = iota((QBLK, 1), 0), iota((1, QBLK), 1)
+        row, col = [one % SOURCES * MOST + one // SOURCES for one in (row, col)]
+        later = col > row
         ones = jnp.ones((stop, HEAD), BF16)
         for c in range(SHARE):
             q = jnp.concatenate([q_scr[c], unit], axis=1)
@@ -343,23 +365,29 @@
             mixed = dot(weights.astype(BF16), v)
             o_scr[c] = (mixed[:, :HEAD] / mixed[:, HEAD:]).astype(BF16)
 
+    def store_all():
+        for block in range(SOURCES // CHUNK):
+            begin = block * CHUNK
+            shape = (CHUNK, SHARE, HEAD)
+            firsts = dot(turn_back, o_scr[:, begin : begin + CHUNK, :].reshape(size, HEAD))
+            begin = begin + SOURCES
+            chosen = bits(back_place == code_scr[block])
+            seconds = lax.dot_general(
+                chosen,
+                o_scr[:, begin : begin + CHUNK, :].reshape(size, HEAD),
+                (((0,), (0,)), ((), ())),
+                preferred_element_type=F32,
+            )
+            both = jnp.concatenate([firsts.reshape(shape), seconds.reshape(shape)], axis=1)
+            out_ref[block * CHUNK : (block + 1) * CHUNK, :, :] = both.astype(BF16)
+
+    def work(number):
+        load_all(number * QBLK)
+        queries_of(number)
+        store_all()
+
     for block in range(ROWS // QBLK):
-        pl.when(step == block)(lambda block=block: queries_of(block))
-
-    for block in range(SOURCES // CHUNK):
-        begin = block * CHUNK
-        shape = (CHUNK, SHARE, HEAD)
-        firsts = dot(turn_back, o_scr[:, begin : begin + CHUNK, :].reshape(size, HEAD))
-        begin = begin + SOURCES
-        chosen = bits(back_place == code_scr[block])
-        seconds = lax.dot_general(
-            chosen,
-            o_scr[:, begin : begin + CHUNK, :].reshape(size, HEAD),
-            (((0,), (0,)), ((), ())),
-            preferred_element_type=F32,
-        )
-        both = jnp.concatenate([firsts.reshape(shape), seconds.reshape(shape)], axis=1)
-        out_ref[block * CHUNK : (block + 1) * CHUNK, :, :] = both.astype(BF16)
+        pl.when(step == block)(lambda block=block: work(block))
 
 
 def lean_attend(received):
@@ -368,8 +396,14 @@
         lean_attend_kernel,
         grid=(ROWS // QBLK,),
         in_specs=[pl.BlockSpec((SOURCES, MESSAGE, HEAD), lambda b: (b, 0, 0))],
-        out_specs=pl.BlockSpec((SOURCES, UNIT, HEAD), lambda b: (b, 0, 0)),
-        out_shape=jax.ShapeDtypeStruct((DEVICES, UNIT, HEAD), BF16),
+        out_specs=[
+            pl.BlockSpec((SOURCES, UNIT, HEAD), lambda b: (b, 0, 0)),
+            pl.BlockSpec((8, HEAD), lambda b: (0, 0)),
+        ],
+        out_shape=[
+            jax.ShapeDtypeStruct((DEVICES, UNIT, HEAD), BF16),
+            jax.ShapeDtypeStruct((8, HEAD), F32),
+        ],
         scratch_shapes=[
             pltpu.VMEM((SHARE, ROWS, 2 * HEAD), BF16),
             pltpu.VMEM((SHARE, ROWS, HEAD), BF16),
@@ -382,10 +416,13 @@
     )(received)
 
 
-def lean_unpack_kernel(row_ref, in_ref, out_ref):
-    row, group, second, rank = token_ranks(row_ref[...])
-    slot = group * UNIT + jnp.where(second > 0.5, SHARE + rank, row - group * SHARE)
-    onehot = bits(iota((CLUSTERS // SHARE * UNIT, TOK), 0).astype(F32) == slot)
+def lean_unpack_kernel(row_ref, in_ref, out_ref, onehot_scr):
+    @pl.when(pl.program_id(0) == 0)
+    def prepare():
+        row, group, second, rank = token_ranks(row_ref[...])
+        slot = group * UNIT + jnp.where(second > 0.5, SHARE + rank, row - group * SHARE)
+        onehot_scr[...] = bits(iota(onehot_scr.shape, 0).astype(F32) == slot)
+
     rows = jnp.concatenate(
         [
             jnp.concatenate([in_ref[j, h] for h in range(SHARE)], axis=1)
@@ -394,7 +431,7 @@
         axis=0,
     )
     out_ref[...] = lax.dot_general(
-        onehot, rows, (((0,), (0,)), ((), ())), preferred_element_type=F32
+        onehot_scr[...], rows, (((0,), (0,)), ((), ())), preferred_element_type=F32
     ).astype(BF16)
 
 
@@ -409,7 +446,8 @@
         ],
         out_specs=pl.BlockSpec((TOK, SHARE * HEAD), lambda g: (0, g)),
         out_shape=jax.ShapeDtypeStruct((TOK, HEADS * HEAD), BF16),
-        compiler_params=pltpu.CompilerParams(vmem_limit_bytes=VMEM),
+        scratch_shapes=[pltpu.VMEM((groups * UNIT, TOK), BF16)],
+        compiler_params=pltpu.CompilerParams(vmem_limit_bytes=63 * 1024 * 1024),
         name="lean_unpack",
     )(row, back)
 
@@ -422,18 +460,19 @@
     row = cluster_ids.reshape(1, TOK)
     sent = lean_pack(row, queries, keys, values)
     received = exchange(sent.reshape(DEVICES, MESSAGE, HEAD))
-    short = jnp.max(received[:, 2 * SHARE + TAIL - 1, SHARE]) > 0
-
-    def lean(received, row, queries, keys, values):
-        back = exchange(lean_attend(received))
+    mixed, flags = lean_attend(received)
+    back = exchange(mixed)
+    short = flags[0, SHARE] > 0.5
+
+    def lean(back, row, queries, keys, values):
         return lean_unpack(row, back.reshape(CLUSTERS // SHARE, HEADS, UNIT, HEAD))
 
-    def full(received, row, queries, keys, values):
+    def full(back, row, queries, keys, values):
         sent = pack(row, queries, keys, values)
         back = exchange(attend(exchange(sent.reshape(DEVICES, 3 * UNIT, HEAD))))
         return unpack(row, back.reshape(CLUSTERS, GROUPS, UNIT, HEAD))
 
-    return lax.cond(short, full, lean, received, row, queries, keys, values)
+    return lax.cond(short, full, lean, back, row, queries, keys, values)
 
 
 def solution(mesh):

time: 242 us -> 235 us (0.971)
  blocking collectives: 65.1 us -> 142 us
  waiting for transfers between devices: 118 us -> 49.8 us
  starting transfers between devices: 24 us -> 13.2 us
  other arithmetic: 2.44 us -> 0 us
    all_to_all x1, blocking collectives: 65.1 us -> 142 us  [exchange(): lax.all_to_all(data, ('seq', 'blk'), split_axis=0, concat_axis=0, tiled=T...]
    all_to_all x1, waiting for transfers between devices: 118 us -> 49.8 us  [exchange(): lax.all_to_all(data, ('seq', 'blk'), split_axis=0, concat_axis=0, tiled=T...]
    all_to_all x1, starting transfers between devices: 24 us -> 13.2 us  [exchange(): lax.all_to_all(data, ('seq', 'blk'), split_axis=0, concat_axis=0, tiled=T...]
    reduce_max x1 -> x0, other arithmetic: 2.44 us -> none  [body(): short = jnp.max(received[:, 2 * SHARE + TAIL - 1, SHARE]) > 0]
  transfers between devices with their start and end apart: 1 -> 1, of which waited for: 1 -> 1; matrix products, arithmetic and copies ran while one was open for 0% -> 1% of each run, Pallas kernels for 0% -> 0%
where the time goes in v4:
time: 235 us
  blocking collectives  142 us (60%)
  waiting for transfers between devices  49.8 us (21%)
  Pallas kernels  27.6 us (12%)
  starting transfers between devices  13.2 us (6%)
    all_to_all x1, blocking collectives, exchange(): lax.all_to_all(data, ('seq', 'blk'), split_axis=0, concat_axis=0, tiled=T...  142 us
    all_to_all x1, waiting for transfers between devices, exchange(): lax.all_to_all(data, ('seq', 'blk'), split_axis=0, concat_axis=0, tiled=T...  49.8 us
    pallas_call x1, Pallas kernels, lean_attend(): pl.pallas_call(lean_attend_kernel, grid=(ROWS // QBLK,), in_specs=[pl.Blo...  17.1 us
    all_to_all x1, starting transfers between devices, exchange(): lax.all_to_all(data, ('seq', 'blk'), split_axis=0, concat_axis=0, tiled=T...  13.2 us
    pallas_call x1, Pallas kernels, lean_pack(): pl.pallas_call(lean_pack_kernel, grid=(GROUPS,), in_specs=[pl.BlockSpec((...  6.29 us
  transfers between devices with their start and end apart: 1, of which 1 were waited for; matrix products, arithmetic and copies ran while one was open for 1% of the time, Pallas kernels for 0%

profile of v4, /device:TPU:1, one launch (start us, length us, event | category | flops | bytes accessed | tf_op | source)
XLA Modules:
  0.0 235.1 jit_solution(4638276174215883204)
XLA Ops:
  0.0 6.3 %lean_pack.1 = bf16[16,32,40,128]{3,2,1,0:T(8,128)(2,1)} custom-call(s32[1,128]{1,0:T(1,128)} %bitcast.9, bf16[128,4096]{1,0:T(8,128)(2,1)} %q_ref.1, bf16[128,4096]{1,0:T(8,128)(2,1)} %k_ref.1, bf16[128,4096]{1,0:T(8,128)(2,1)} %v_ref.1), custom_call_target="tpu_custom_call" | custom-call | tf_op jit(solution)/shard_map/lean_pack/pallas_call | solution.py:279
  6.3 142.4 %all_to_all.20.in_ref = bf16[512,40,128]{2,1,0:T(8,128)(2,1)} all-to-all(bf16[512,40,128]{2,1,0:T(8,128)(2,1)} %bitcast.7), channel_id=1, replica_groups=mesh['seq'=128,'blk'=4] {'seq','blk'}, dimensions={0} | all-to-all | bytes 10485760 | tf_op jit(solution)/shard_map/all_to_all | solution.py:456
  148.7 0.0 copy-start
  148.7 17.1 %lean_attend.1 = (bf16[512,16,128]{2,1,0:T(8,128)(2,1)}, f32[8,128]{1,0:T(8,128)}) custom-call(bf16[512,40,128]{2,1,0:T(8,128)(2,1)} %all_to_all.20.in_ref), custom_call_target="tpu_custom_call" | custom-call | tf_op jit(solution)/shard_map/lean_attend/pallas_call | solution.py:395
  165.7 13.2 %all-to-all-start.3 = ((bf16[512,16,128]{2,1,0:T(8,128)(2,1)}), bf16[512,16,128]{2,1,0:T(8,128)(2,1)}, u32[]{:S(2)}, u32[]{:S(2)}) async-start(bf16[512,16,128]{2,1,0:T(8,128)(2,1)} %get-tuple-element.29), calls=%async_computation.3 | async-start | bytes 4194304 | tf_op jit(solution)/shard_map/all_to_all | solution.py:456
  178.9 1.3 slice.3
  181.0 49.8 %all-to-all-done.3 = bf16[512,16,128]{2,1,0:T(8,128)(2,1)} async-done(((bf16[512,16,128]{2,1,0:T(8,128)(2,1)}), bf16[512,16,128]{2,1,0:T(8,128)(2,1)}, u32[]{:S(2)}, u32[]{:S(2)}) %all-to-all-start.3) | async-done | bytes 2097184 | tf_op jit(solution)/shard_map/all_to_all | solution.py:456
  230.8 0.0 copy-done
  230.8 4.2 %conditional.1 = (bf16[128,4096]{1,0:T(8,128)(2,1)}) conditional(s32[]{:T(128)} %bitcast.5, (bf16[512,16,128]{2,1,0:T(8,128)(2,1)}, s32[1,128]{1,0:T(1,128)S(1)}) %tuple.17, (s32[1,128]{1,0:T(1,128)S(1)}, bf16[128,4096]{1,0:T(8,128)(2,1)}, bf16[128,4096]{1,0:T(8,128)(2,1)}, bf16[128,4096]{1,0:T(8,128)(2,1)}) %tuple.18), branch_computations={%region_0.0_spmd, %region_1.0_spmd} | conditional | bytes 16777224 | solution.py:475
  230.8 4.2 %lean_unpack.1 = bf16[128,4096]{1,0:T(8,128)(2,1)} custom-call(s32[1,128]{1,0:T(1,128)S(1)} %get-tuple-element.20.row_ref, bf16[16,32,16,128]{3,2,1,0:T(8,128)(2,1)} %bitcast.in_ref), custom_call_target="tpu_custom_call" | custom-call | tf_op jit(solution)/shard_map/cond/branch_0_fun/lean_unpack/pallas_call | solution.py:440
Async XLA Ops:
  148.7 82.2 %copy-start = (s32[128,1]{0,1:T(1,128)S(1)}, s32[128,1]{0,1:T(1,128)}, u32[]{:S(2)}) copy-start(s32[128,1]{0,1:T(1,128)} %param.9) | copy-start | bytes 1540
  165.7 65.1 %all-to-all-start.3 = ((bf16[512,16,128]{2,1,0:T(8,128)(2,1)}), bf16[512,16,128]{2,1,0:T(8,128)(2,1)}, u32[]{:S(2)}, u32[]{:S(2)}) async-start(bf16[512,16,128]{2,1,0:T(8,128)(2,1)} %get-tuple-element.29), calls=%async_computation.3 | async-start | bytes 4194304 | tf_op jit(solution)/shard_map/all_to_all | solution.py:456

commit v5 on v4

--- a/solution.py
+++ b/solution.py
@@ -19,9 +19,13 @@
 SOURCES = QBLK // MOST
 CHUNK = 16
 VMEM = 56 * 1024 * 1024
+PAIR = 2
+POOL = PAIR * SHARE
 EXTRA = 5
 TAIL = 16
-MESSAGE = 3 * SHARE + TAIL
+HALF = TAIL // PAIR
+MESSAGE = 3 * SHARE + HALF
+CHIPS = 4
 NONE = -64.0
 EMPTY = 256.0
 MASKED = -1e30
@@ -217,7 +221,7 @@
     same = col == row
     second = jnp.sum((same & (above < across)).astype(F32), axis=0, keepdims=True)
     second_col = jnp.sum((same & (across < above)).astype(F32), axis=1, keepdims=True)
-    group, group_col = jnp.floor(row / SHARE), jnp.floor(col / SHARE)
+    group, group_col = jnp.floor(row / POOL), jnp.floor(col / POOL)
     lower = (second_col > 0.5) & (group_col == group) & (col < row)
     rank = jnp.sum(lower.astype(F32), axis=0, keepdims=True)
     return row, group, second, rank
@@ -244,12 +248,12 @@
         there = jnp.sum(seconds, axis=1, keepdims=True) > 0.5
         code = jnp.where(there, jnp.sum(seconds * rank, axis=1, keepdims=True), NONE)
         short = jnp.max(second * (rank + 1.0), axis=1, keepdims=True) > EXTRA + 0.5
-        place, lane = iota((CLUSTERS, HEAD), 0) % SHARE, iota((CLUSTERS, HEAD), 1)
+        place, lane = iota((CLUSTERS, HEAD), 0) % POOL, iota((CLUSTERS, HEAD), 1)
         codes = jnp.where(lane == place, code, 0.0)
-        codes = jnp.where((lane == SHARE) & short, 1.0, codes).astype(BF16)
-        size = CLUSTERS // SHARE * TAIL
+        codes = jnp.where((lane == POOL) & short, 1.0, codes).astype(BF16)
+        size = CLUSTERS // POOL * TAIL
         number = iota((size, CLUSTERS), 0)
-        last = (number % TAIL == TAIL - 1) & (number // TAIL == iota((size, CLUSTERS), 1) // SHARE)
+        last = (number % TAIL == TAIL - 1) & (number // TAIL == iota((size, CLUSTERS), 1) // POOL)
         notes_scr[...] = dot(bits(last), codes)
 
         fits = is_second & (rank < EXTRA - 0.5)
@@ -267,44 +271,51 @@
     for j in range(CLUSTERS // SHARE):
         rows = slice(j * SHARE, (j + 1) * SHARE)
         message = jnp.concatenate(
-            [q[rows], k[rows], tail[j * TAIL : (j + 1) * TAIL], v[rows]], axis=0
+            [q[rows], k[rows], v[rows], tail[j * HALF : (j + 1) * HALF]], axis=0
         ).astype(BF16)
         for h in range(SHARE):
-            out_ref[j, h] = message[:, h * HEAD : (h + 1) * HEAD]
+            place = (j // PAIR, h // CHIPS, j % PAIR, h % CHIPS)
+            out_ref[place] = message[:, h * HEAD : (h + 1) * HEAD]
 
 
 def lean_pack(row, queries, keys, values):
     data = pl.BlockSpec((TOK, SHARE * HEAD), lambda g: (0, g))
-    groups = CLUSTERS // SHARE
+    shape = (CLUSTERS // POOL, HEADS // CHIPS, PAIR, CHIPS, MESSAGE, HEAD)
+    block = shape[:1] + (SHARE // CHIPS,) + shape[2:]
+    tails = CLUSTERS // POOL * TAIL
     return pl.pallas_call(
         lean_pack_kernel,
         grid=(GROUPS,),
         in_specs=[pl.BlockSpec((1, TOK), lambda g: (0, 0)), data, data, data],
-        out_specs=pl.BlockSpec((groups, SHARE, MESSAGE, HEAD), lambda g: (0, g, 0, 0)),
-        out_shape=jax.ShapeDtypeStruct((groups, HEADS, MESSAGE, HEAD), BF16),
+        out_specs=pl.BlockSpec(block, lambda g: (0, g, 0, 0, 0, 0)),
+        out_shape=jax.ShapeDtypeStruct(shape, BF16),
         scratch_shapes=[
             pltpu.VMEM((CLUSTERS, TOK), BF16),
             pltpu.VMEM((CLUSTERS, HEAD), F32),
-            pltpu.VMEM((groups * TAIL, HEAD), F32),
-            pltpu.VMEM((groups * TAIL, 3 * TOK), BF16),
+            pltpu.VMEM((tails, HEAD), F32),
+            pltpu.VMEM((tails, 3 * TOK), BF16),
         ],
         compiler_params=pltpu.CompilerParams(vmem_limit_bytes=VMEM),
         name="lean_pack",
     )(row, queries, keys, values)
 
 
-def lean_attend_kernel(in_ref, out_ref, flag_ref, k_scr, v_scr, q_scr, o_scr, code_scr):
+def lean_attend_kernel(
+    side_ref, in_ref, other_ref, out_ref, flag_ref, k_scr, v_scr, q_scr, o_scr, code_scr
+):
     step = pl.program_id(0)
+    side = side_ref[0]
     size = SHARE * CHUNK
     row, col = iota((size, size), 0), iota((size, size), 1)
     turn = bits(col == row % CHUNK * SHARE + row // CHUNK)
     turn_back = bits(row == col % CHUNK * SHARE + col // CHUNK)
     lane = iota((size, HEAD), 1)
-    own_lane = lane == iota((size, HEAD), 0) // CHUNK
+    own_lane = lane == iota((size, HEAD), 0) // CHUNK + side * SHARE
     wide_row, wide_col = iota((size, CHUNK * TAIL), 0), iota((size, CHUNK * TAIL), 1)
     own_tail = wide_row % CHUNK == wide_col // TAIL
-    pick_notes = bits(own_tail & (wide_col % TAIL == TAIL - 1))
-    tail_place = jnp.where(own_tail, (wide_col % TAIL).astype(F32), -200.0)
+    wide_col = (wide_col + side * HALF) % TAIL
+    pick_notes = bits(own_tail & (wide_col == TAIL - 1))
+    tail_place = jnp.where(own_tail, wide_col.astype(F32), -200.0)
     back_place = jnp.where(row % CHUNK == col // SHARE, (col % SHARE).astype(F32), -200.0)
 
     def keep(part, start, q, k, v):
@@ -319,14 +330,15 @@
         flags = jnp.zeros((size, HEAD), F32)
         for block in range(SOURCES // CHUNK):
             part = in_ref[block * CHUNK : (block + 1) * CHUNK, :, :].astype(F32)
-            at = 2 * SHARE
-            pieces = [part[:, :SHARE], part[:, SHARE:at], part[:, at + TAIL :]]
-            tall = jnp.concatenate([one.reshape(size, HEAD) for one in pieces], axis=1)
+            pieces = [part[:, i * SHARE : (i + 1) * SHARE].reshape(size, HEAD) for i in range(3)]
+            tall = jnp.concatenate(pieces, axis=1)
             mixed = dot(turn, tall.astype(BF16))
             start = here + block * CHUNK
             keep(block * CHUNK, start, mixed[:, :HEAD], mixed[:, HEAD : 2 * HEAD], mixed[:, 2 * HEAD :])
 
-            tail = part[:, at : at + TAIL].reshape(CHUNK * TAIL, HEAD).astype(BF16)
+            other = other_ref[block * CHUNK : (block + 1) * CHUNK, :, :].astype(F32)
+            tail = jnp.concatenate([part[:, 3 * SHARE :], other], axis=1)
+            tail = tail.reshape(CHUNK * TAIL, HEAD).astype(BF16)
             notes = dot(pick_notes, tail)
             flags = jnp.maximum(flags, notes)
             code = jnp.sum(jnp.where(own_lane, notes, 0.0), axis=1, keepdims=True)
@@ -390,12 +402,16 @@
         pl.when(step == block)(lambda block=block: work(block))
 
 
-def lean_attend(received):
+def lean_attend(side, received, other):
     part = pltpu.VMEM((SHARE, QBLK, HEAD), BF16)
     return pl.pallas_call(
         lean_attend_kernel,
         grid=(ROWS // QBLK,),
-        in_specs=[pl.BlockSpec((SOURCES, MESSAGE, HEAD), lambda b: (b, 0, 0))],
+        in_specs=[
+            pl.BlockSpec(memory_space=pltpu.SMEM),
+            pl.BlockSpec((SOURCES, MESSAGE, HEAD), lambda b: (b, 0, 0)),
+            pl.BlockSpec((SOURCES, HALF, HEAD), lambda b: (b, 0, 0)),
+        ],
         out_specs=[
             pl.BlockSpec((SOURCES, UNIT, HEAD), lambda b: (b, 0, 0)),
             pl.BlockSpec((8, HEAD), lambda b: (0, 0)),
@@ -413,19 +429,22 @@
         ],
         compiler_params=pltpu.CompilerParams(vmem_limit_bytes=VMEM),
         name="lean_attend",
-    )(received)
+    )(side, received, other)
 
 
 def lean_unpack_kernel(row_ref, in_ref, out_ref, onehot_scr):
     @pl.when(pl.program_id(0) == 0)
     def prepare():
-        row, group, second, rank = token_ranks(row_ref[...])
-        slot = group * UNIT + jnp.where(second > 0.5, SHARE + rank, row - group * SHARE)
+        row, _, second, rank = token_ranks(row_ref[...])
+        owner = jnp.floor(row / SHARE)
+        slot = owner * UNIT + jnp.where(second > 0.5, SHARE + rank, row - owner * SHARE)
         onehot_scr[...] = bits(iota(onehot_scr.shape, 0).astype(F32) == slot)
 
     rows = jnp.concatenate(
         [
-            jnp.concatenate([in_ref[j, h] for h in range(SHARE)], axis=1)
+            jnp.concatenate(
+                [in_ref[j // PAIR, h // CHIPS, j % PAIR, h % CHIPS] for h in range(SHARE)], axis=1
+            )
             for j in range(CLUSTERS // SHARE)
         ],
         axis=0,
@@ -436,17 +455,17 @@
 
 
 def lean_unpack(row, back):
-    groups = CLUSTERS // SHARE
+    block = (CLUSTERS // POOL, SHARE // CHIPS, PAIR, CHIPS, UNIT, HEAD)
     return pl.pallas_call(
         lean_unpack_kernel,
         grid=(GROUPS,),
         in_specs=[
             pl.BlockSpec((1, TOK), lambda g: (0, 0)),
-            pl.BlockSpec((groups, SHARE, UNIT, HEAD), lambda g: (0, g, 0, 0)),
+            pl.BlockSpec(block, lambda g: (0, g, 0, 0, 0, 0)),
         ],
         out_specs=pl.BlockSpec((TOK, SHARE * HEAD), lambda g: (0, g)),
         out_shape=jax.ShapeDtypeStruct((TOK, HEADS * HEAD), BF16),
-        scratch_shapes=[pltpu.VMEM((groups * UNIT, TOK), BF16)],
+        scratch_shapes=[pltpu.VMEM((CLUSTERS // SHARE * UNIT, TOK), BF16)],
         compiler_params=pltpu.CompilerParams(vmem_limit_bytes=63 * 1024 * 1024),
         name="lean_unpack",
     )(row, back)
@@ -460,12 +479,16 @@
     row = cluster_ids.reshape(1, TOK)
     sent = lean_pack(row, queries, keys, values)
     received = exchange(sent.reshape(DEVICES, MESSAGE, HEAD))
-    mixed, flags = lean_attend(received)
+    swap = [(i, i ^ 1) for i in range(CLUSTERS)]
+    other = lax.ppermute(received[:, 3 * SHARE :, :], "seq", swap)
+    side = (lax.axis_index("seq") % PAIR).astype(jnp.int32).reshape(1)
+    mixed, flags = lean_attend(side, received, other)
     back = exchange(mixed)
-    short = flags[0, SHARE] > 0.5
+    short = flags[0, POOL] > 0.5
 
     def lean(back, row, queries, keys, values):
-        return lean_unpack(row, back.reshape(CLUSTERS // SHARE, HEADS, UNIT, HEAD))
+        back = back.reshape(CLUSTERS // POOL, HEADS // CHIPS, PAIR, CHIPS, UNIT, HEAD)
+        return lean_unpack(row, back)
 
     def full(back, row, queries, keys, values):
         sent = pack(row, queries, keys, values)

time: 235 us -> 220 us (0.936)
  blocking collectives: 142 us -> 120 us
  local copies, waits for them, and re-layouts: 1.35 us -> 4.31 us
  waiting for transfers between devices: 49.8 us -> 52.2 us
  starting transfers between devices: 13.2 us -> 15.6 us
    all_to_all x1, blocking collectives: 142 us -> 120 us  [exchange(): lax.all_to_all(data, ('seq', 'blk'), split_axis=0, concat_axis=0, tiled=T...]
    unnamed x2 -> x6, local copies, waits for them, and re-layouts: 0.01 us -> 2.92 us
    ppermute x0 -> x1, starting transfers between devices: none -> 2.59 us  [body(): other = lax.ppermute(received[:, 3 * SHARE:, :], 'seq', swap)]
  transfers between devices with their start and end apart: 1 -> 2, of which waited for: 1 -> 2; matrix products, arithmetic and copies ran while one was open for 1% -> 1% of each run, Pallas kernels for 0% -> 0%
where the time goes in v5:
time: 220 us
  blocking collectives  120 us (55%)
  waiting for transfers between devices  52.2 us (24%)
  Pallas kernels  27 us (12%)
  starting transfers between devices  15.6 us (7%)
  local copies, waits for them, and re-layouts  4.31 us (2%)
    all_to_all x1, blocking collectives, exchange(): lax.all_to_all(data, ('seq', 'blk'), split_axis=0, concat_axis=0, tiled=T...  120 us
    all_to_all x1, waiting for transfers between devices, exchange(): lax.all_to_all(data, ('seq', 'blk'), split_axis=0, concat_axis=0, tiled=T...  50 us
    pallas_call x1, Pallas kernels, lean_attend(): pl.pallas_call(lean_attend_kernel, grid=(ROWS // QBLK,), in_specs=[pl.Blo...  17 us
    all_to_all x1, starting transfers between devices, exchange(): lax.all_to_all(data, ('seq', 'blk'), split_axis=0, concat_axis=0, tiled=T...  13 us
    pallas_call x1, Pallas kernels, lean_pack(): pl.pallas_call(lean_pack_kernel, grid=(GROUPS,), in_specs=[pl.BlockSpec((...  5.71 us
  transfers between devices with their start and end apart: 2, of which 2 were waited for; matrix products, arithmetic and copies ran while one was open for 1% of the time, Pallas kernels for 0%

profile of v5, /device:TPU:1, one launch (start us, length us, event | category | flops | bytes accessed | tf_op | source)
XLA Modules:
  0.0 219.6 jit_solution(368954650105157990)
XLA Ops:
  0.0 5.7 %lean_pack.1 = bf16[8,8,2,4,32,128]{5,4,3,2,1,0:T(8,128)(2,1)} custom-call(s32[1,128]{1,0:T(1,128)} %bitcast.10, bf16[128,4096]{1,0:T(8,128)(2,1)} %q_ref.1, bf16[128,4096]{1,0:T(8,128)(2,1)} %k_ref.1, bf16[128,4096]{1,0:T(8,128)(2,1)} %v_ref.1), custom_call_target="tpu_custom_call" | custom-call | tf_op jit(solution)/shard_map/lean_pack/pallas_call | solution.py:286
  5.7 119.8 %all_to_all.20.in_ref = bf16[512,32,128]{2,1,0:T(8,128)(2,1)S(1)} all-to-all(bf16[512,32,128]{2,1,0:T(8,128)(2,1)} %bitcast.8), channel_id=1, replica_groups=mesh['seq'=128,'blk'=4] {'seq','blk'}, dimensions={0} | all-to-all | bytes 8388608 | tf_op jit(solution)/shard_map/all_to_all | solution.py:475
  125.5 0.0 copy-start
  125.5 1.9 copy-done
  127.5 0.1 slice.8
  127.6 2.6 %collective-permute-start = (bf16[512,8,128]{2,1,0:T(8,128)(2,1)S(1)}, bf16[512,8,128]{2,1,0:T(8,128)(2,1)S(1)}, u32[]{:S(2)}, u32[]{:S(2)}) collective-permute-start(bf16[512,8,128]{2,1,0:T(8,128)(2,1)S(1)} %slice.8), channel_id=1, source_target_pairs={{0,4},{4,0},{8,12},{12,8},{16,20},{20,16},{24,28},{28,24},{32,36},... | collective-permute-start | bytes 3145736 | tf_op jit(solution)/shard_map/ppermute | solution.py:483
  130.2 2.3 %collective-permute-done.other_ref = bf16[512,8,128]{2,1,0:T(8,128)(2,1)S(1)} collective-permute-done((bf16[512,8,128]{2,1,0:T(8,128)(2,1)S(1)}, bf16[512,8,128]{2,1,0:T(8,128)(2,1)S(1)}, u32[]{:S(2)}, u32[]{:S(2)}) %collective-permute-start) | collective-permute-done | bytes 1048608 | tf_op jit(solution)/shard_map/ppermute | solution.py:483
  132.5 0.0 copy-start.1
  132.5 1.0 copy-done.1
  133.5 0.0 copy-start.2
  133.5 17.0 %lean_attend.1 = (bf16[512,16,128]{2,1,0:T(8,128)(2,1)}, f32[8,128]{1,0:T(8,128)}) custom-call(s32[1]{0:T(128)} %bitcast.3.side_ref, bf16[512,32,128]{2,1,0:T(8,128)(2,1)} %copy-done, bf16[512,8,128]{2,1,0:T(8,128)(2,1)} %copy-done.1), custom_call_target="tpu_custom_call" | custom-call | tf_op jit(solution)/shard_map/lean_attend/pallas_call | solution.py:407
  150.5 13.0 %all-to-all-start.3 = ((bf16[512,16,128]{2,1,0:T(8,128)(2,1)}), bf16[512,16,128]{2,1,0:T(8,128)(2,1)}, u32[]{:S(2)}, u32[]{:S(2)}) async-start(bf16[512,16,128]{2,1,0:T(8,128)(2,1)} %get-tuple-element.29), calls=%async_computation.3 | async-start | bytes 4194304 | tf_op jit(solution)/shard_map/all_to_all | solution.py:475
  163.5 1.3 slice.7
  165.4 50.0 %all-to-all-done.3 = bf16[512,16,128]{2,1,0:T(8,128)(2,1)} async-done(((bf16[512,16,128]{2,1,0:T(8,128)(2,1)}), bf16[512,16,128]{2,1,0:T(8,128)(2,1)}, u32[]{:S(2)}, u32[]{:S(2)}) %all-to-all-start.3) | async-done | bytes 2097184 | tf_op jit(solution)/shard_map/all_to_all | solution.py:475
  215.4 0.0 copy-done.2
  215.4 4.2 %conditional.1 = (bf16[128,4096]{1,0:T(8,128)(2,1)}) conditional(s32[]{:T(128)} %bitcast.6, (bf16[512,16,128]{2,1,0:T(8,128)(2,1)}, s32[1,128]{1,0:T(1,128)S(1)}) %tuple.17, (s32[1,128]{1,0:T(1,128)S(1)}, bf16[128,4096]{1,0:T(8,128)(2,1)}, bf16[128,4096]{1,0:T(8,128)(2,1)}, bf16[128,4096]{1,0:T(8,128)(2,1)}) %tuple.18), branch_computations={%region_0.1_spmd, %region_1.2_spmd} | conditional | bytes 16777224 | solution.py:498
  215.4 4.2 %lean_unpack.1 = bf16[128,4096]{1,0:T(8,128)(2,1)} custom-call(s32[1,128]{1,0:T(1,128)S(1)} %get-tuple-element.20.row_ref, bf16[8,8,2,4,16,128]{5,4,3,2,1,0:T(8,128)(2,1)} %bitcast.in_ref), custom_call_target="tpu_custom_call" | custom-call | tf_op jit(solution)/shard_map/cond/branch_0_fun/lean_unpack/pallas_call | solution.py:459
Async XLA Ops:
  125.5 1.9 copy-start
  127.6 4.9 %collective-permute-start = (bf16[512,8,128]{2,1,0:T(8,128)(2,1)S(1)}, bf16[512,8,128]{2,1,0:T(8,128)(2,1)S(1)}, u32[]{:S(2)}, u32[]{:S(2)}) collective-permute-start(bf16[512,8,128]{2,1,0:T(8,128)(2,1)S(1)} %slice.8), channel_id=1, source_target_pairs={{0,4},{4,0},{8,12},{12,8},{16,20},{20,16},{24,28},{28,24},{32,36},... | collective-permute-start | bytes 3145736 | tf_op jit(solution)/shard_map/ppermute | solution.py:483
  132.5 1.0 copy-start.1
  133.5 81.9 %copy-start.2 = (s32[128,1]{0,1:T(1,128)S(1)}, s32[128,1]{0,1:T(1,128)}, u32[]{:S(2)}) copy-start(s32[128,1]{0,1:T(1,128)} %param.9) | copy-start | bytes 1540
  150.5 64.9 %all-to-all-start.3 = ((bf16[512,16,128]{2,1,0:T(8,128)(2,1)}), bf16[512,16,128]{2,1,0:T(8,128)(2,1)}, u32[]{:S(2)}, u32[]{:S(2)}) async-start(bf16[512,16,128]{2,1,0:T(8,128)(2,1)} %get-tuple-element.29), calls=%async_computation.3 | async-start | bytes 4194304 | tf_op jit(solution)/shard_map/all_to_all | solution.py:475

commit v6 on v5

--- a/solution.py
+++ b/solution.py
@@ -26,6 +26,7 @@
 HALF = TAIL // PAIR
 MESSAGE = 3 * SHARE + HALF
 CHIPS = 4
+WIDE = 16
 NONE = -64.0
 EMPTY = 256.0
 MASKED = -1e30
@@ -265,27 +266,27 @@
 
     data = [ref[...] for ref in (q_ref, k_ref, v_ref)]
     tail = dot(chosen_scr[...], jnp.concatenate(data, axis=0))
-    tail = tail + jnp.concatenate([notes_scr[...]] * SHARE, axis=1)
+    tail = tail + jnp.concatenate([notes_scr[...]] * WIDE, axis=1)
     q, k, v = [dot(first_scr[...], one) for one in data]
-    k = k + jnp.concatenate([empty_scr[...]] * SHARE, axis=1)
+    k = k + jnp.concatenate([empty_scr[...]] * WIDE, axis=1)
     for j in range(CLUSTERS // SHARE):
         rows = slice(j * SHARE, (j + 1) * SHARE)
         message = jnp.concatenate(
             [q[rows], k[rows], v[rows], tail[j * HALF : (j + 1) * HALF]], axis=0
         ).astype(BF16)
-        for h in range(SHARE):
+        for h in range(WIDE):
             place = (j // PAIR, h // CHIPS, j % PAIR, h % CHIPS)
             out_ref[place] = message[:, h * HEAD : (h + 1) * HEAD]
 
 
 def lean_pack(row, queries, keys, values):
-    data = pl.BlockSpec((TOK, SHARE * HEAD), lambda g: (0, g))
+    data = pl.BlockSpec((TOK, WIDE * HEAD), lambda g: (0, g))
     shape = (CLUSTERS // POOL, HEADS // CHIPS, PAIR, CHIPS, MESSAGE, HEAD)
-    block = shape[:1] + (SHARE // CHIPS,) + shape[2:]
+    block = shape[:1] + (WIDE // CHIPS,) + shape[2:]
     tails = CLUSTERS // POOL * TAIL
     return pl.pallas_call(
         lean_pack_kernel,
-        grid=(GROUPS,),
+        grid=(HEADS // WIDE,),
         in_specs=[pl.BlockSpec((1, TOK), lambda g: (0, 0)), data, data, data],
         out_specs=pl.BlockSpec(block, lambda g: (0, g, 0, 0, 0, 0)),
         out_shape=jax.ShapeDtypeStruct(shape, BF16),
@@ -427,7 +428,7 @@
             part,
             pltpu.VMEM((SOURCES // CHUNK, SHARE * CHUNK, HEAD), F32),
         ],
-        compiler_params=pltpu.CompilerParams(vmem_limit_bytes=VMEM),
+        compiler_params=pltpu.CompilerParams(vmem_limit_bytes=VMEM // 2),
         name="lean_attend",
     )(side, received, other)
 
@@ -443,7 +444,7 @@
     rows = jnp.concatenate(
         [
             jnp.concatenate(
-                [in_ref[j // PAIR, h // CHIPS, j % PAIR, h % CHIPS] for h in range(SHARE)], axis=1
+                [in_ref[j // PAIR, h // CHIPS, j % PAIR, h % CHIPS] for h in range(WIDE)], axis=1
             )
             for j in range(CLUSTERS // SHARE)
         ],
@@ -455,15 +456,15 @@
 
 
 def lean_unpack(row, back):
-    block = (CLUSTERS // POOL, SHARE // CHIPS, PAIR, CHIPS, UNIT, HEAD)
+    block = (CLUSTERS // POOL, WIDE // CHIPS, PAIR, CHIPS, UNIT, HEAD)
     return pl.pallas_call(
         lean_unpack_kernel,
-        grid=(GROUPS,),
+        grid=(HEADS // WIDE,),
         in_specs=[
             pl.BlockSpec((1, TOK), lambda g: (0, 0)),
             pl.BlockSpec(block, lambda g: (0, g, 0, 0, 0, 0)),
         ],
-        out_specs=pl.BlockSpec((TOK, SHARE * HEAD), lambda g: (0, g)),
+        out_specs=pl.BlockSpec((TOK, WIDE * HEAD), lambda g: (0, g)),
         out_shape=jax.ShapeDtypeStruct((TOK, HEADS * HEAD), BF16),
         scratch_shapes=[pltpu.VMEM((CLUSTERS // SHARE * UNIT, TOK), BF16)],
         compiler_params=pltpu.CompilerParams(vmem_limit_bytes=63 * 1024 * 1024),

time: 220 us -> 218 us (level)
  Pallas kernels: 27 us -> 23.6 us
  transfers between devices with their start and end apart: 2 -> 2, of which waited for: 2 -> 2; matrix products, arithmetic and copies ran while one was open for 1% -> 0% of each run, Pallas kernels for 0% -> 0%
where the time goes in v6:
time: 218 us; the launch traced here: 217 us
  blocking collectives  120 us (55%)
  waiting for transfers between devices  52.9 us (24%)
  Pallas kernels  23.6 us (11%)
  starting transfers between devices  15.5 us (7%)
  local copies, waits for them, and re-layouts  4.85 us (2%)
    all_to_all x1, blocking collectives, exchange(): lax.all_to_all(data, ('seq', 'blk'), split_axis=0, concat_axis=0, tiled=T...  120 us
    all_to_all x1, waiting for transfers between devices, exchange(): lax.all_to_all(data, ('seq', 'blk'), split_axis=0, concat_axis=0, tiled=T...  50.7 us
    pallas_call x1, Pallas kernels, lean_attend(): pl.pallas_call(lean_attend_kernel, grid=(ROWS // QBLK,), in_specs=[pl.Blo...  15.7 us
    all_to_all x1, starting transfers between devices, exchange(): lax.all_to_all(data, ('seq', 'blk'), split_axis=0, concat_axis=0, tiled=T...  13 us
    pallas_call x1, Pallas kernels, lean_pack(): pl.pallas_call(lean_pack_kernel, grid=(HEADS // WIDE,), in_specs=[pl.Bloc...  4.94 us
  transfers between devices with their start and end apart: 2, of which 2 were waited for; matrix products, arithmetic and copies ran while one was open for 0% of the time, Pallas kernels for 0%

profile of v6, /device:TPU:1, one launch (start us, length us, event | category | flops | bytes accessed | tf_op | source)
XLA Modules:
  0.0 217.4 jit_solution(213204135080591019)
XLA Ops:
  0.0 4.9 %lean_pack.1 = bf16[8,8,2,4,32,128]{5,4,3,2,1,0:T(8,128)(2,1)} custom-call(s32[1,128]{1,0:T(1,128)} %bitcast.10, bf16[128,4096]{1,0:T(8,128)(2,1)} %q_ref.1, bf16[128,4096]{1,0:T(8,128)(2,1)} %k_ref.1, bf16[128,4096]{1,0:T(8,128)(2,1)} %v_ref.1), custom_call_target="tpu_custom_call" | custom-call | tf_op jit(solution)/shard_map/lean_pack/pallas_call | solution.py:287
  4.9 119.8 %all_to_all.20.in_ref = bf16[512,32,128]{2,1,0:T(8,128)(2,1)S(1)} all-to-all(bf16[512,32,128]{2,1,0:T(8,128)(2,1)} %bitcast.8), channel_id=1, replica_groups=mesh['seq'=128,'blk'=4] {'seq','blk'}, dimensions={0} | all-to-all | bytes 8388608 | tf_op jit(solution)/shard_map/all_to_all | solution.py:476
  124.8 0.1 slice.8
  124.9 0.0 copy-start
  124.9 1.9 copy-done
  126.8 2.6 %collective-permute-start = (bf16[512,8,128]{2,1,0:T(8,128)(2,1)S(1)}, bf16[512,8,128]{2,1,0:T(8,128)(2,1)S(1)}, u32[]{:S(2)}, u32[]{:S(2)}) collective-permute-start(bf16[512,8,128]{2,1,0:T(8,128)(2,1)S(1)} %slice.8), channel_id=1, source_target_pairs={{0,4},{4,0},{8,12},{12,8},{16,20},{20,16},{24,28},{28,24},{32,36},... | collective-permute-start | bytes 3145736 | tf_op jit(solution)/shard_map/ppermute | solution.py:484
  129.4 2.3 %collective-permute-done.other_ref = bf16[512,8,128]{2,1,0:T(8,128)(2,1)S(1)} collective-permute-done((bf16[512,8,128]{2,1,0:T(8,128)(2,1)S(1)}, bf16[512,8,128]{2,1,0:T(8,128)(2,1)S(1)}, u32[]{:S(2)}, u32[]{:S(2)}) %collective-permute-start) | collective-permute-done | bytes 1048608 | tf_op jit(solution)/shard_map/ppermute | solution.py:484
  131.7 0.0 copy-start.1
  131.7 2.2 %copy-done.1 = bf16[512,32,128]{2,1,0:T(8,128)(2,1)S(1)} copy-done((bf16[512,32,128]{2,1,0:T(8,128)(2,1)S(1)}, bf16[512,32,128]{2,1,0:T(8,128)(2,1)}, u32[]{:S(2)}) %copy-start.1) | copy-done | bytes 4194328
  133.9 0.0 copy-start.2
  133.9 15.7 %lean_attend.1 = (bf16[512,16,128]{2,1,0:T(8,128)(2,1)}, f32[8,128]{1,0:T(8,128)S(1)}) custom-call(s32[1]{0:T(128)} %bitcast.3.side_ref, bf16[512,32,128]{2,1,0:T(8,128)(2,1)S(1)} %copy-done.1, bf16[512,8,128]{2,1,0:T(8,128)(2,1)S(1)} %collective-permute-done.other_ref), custom_call_target="tpu_custom_call" | custom-call | tf_op jit(solution)/shard_map/lean_attend/pallas_call | solution.py:408
  149.6 13.0 %all-to-all-start.3 = ((bf16[512,16,128]{2,1,0:T(8,128)(2,1)}), bf16[512,16,128]{2,1,0:T(8,128)(2,1)}, u32[]{:S(2)}, u32[]{:S(2)}) async-start(bf16[512,16,128]{2,1,0:T(8,128)(2,1)} %get-tuple-element.29), calls=%async_computation.3 | async-start | bytes 4194304 | tf_op jit(solution)/shard_map/all_to_all | solution.py:476
  162.6 0.6 slice.7
  163.8 50.7 %all-to-all-done.3 = bf16[512,16,128]{2,1,0:T(8,128)(2,1)} async-done(((bf16[512,16,128]{2,1,0:T(8,128)(2,1)}), bf16[512,16,128]{2,1,0:T(8,128)(2,1)}, u32[]{:S(2)}, u32[]{:S(2)}) %all-to-all-start.3) | async-done | bytes 2097184 | tf_op jit(solution)/shard_map/all_to_all | solution.py:476
  214.5 0.0 copy-done.2
  214.5 2.9 %conditional.1 = (bf16[128,4096]{1,0:T(8,128)(2,1)}) conditional(s32[]{:T(128)} %bitcast.6, (bf16[512,16,128]{2,1,0:T(8,128)(2,1)}, s32[1,128]{1,0:T(1,128)S(1)}) %tuple.17, (s32[1,128]{1,0:T(1,128)S(1)}, bf16[128,4096]{1,0:T(8,128)(2,1)}, bf16[128,4096]{1,0:T(8,128)(2,1)}, bf16[128,4096]{1,0:T(8,128)(2,1)}) %tuple.18), branch_computations={%region_0.1_spmd, %region_1.2_spmd} | conditional | bytes 16777224 | solution.py:499
  214.5 2.9 %lean_unpack.1 = bf16[128,4096]{1,0:T(8,128)(2,1)} custom-call(s32[1,128]{1,0:T(1,128)S(1)} %get-tuple-element.20.row_ref, bf16[8,8,2,4,16,128]{5,4,3,2,1,0:T(8,128)(2,1)} %bitcast.in_ref), custom_call_target="tpu_custom_call" | custom-call | tf_op jit(solution)/shard_map/cond/branch_0_fun/lean_unpack/pallas_call | solution.py:460
Async XLA Ops:
  124.9 1.9 copy-start
  126.8 4.8 %collective-permute-start = (bf16[512,8,128]{2,1,0:T(8,128)(2,1)S(1)}, bf16[512,8,128]{2,1,0:T(8,128)(2,1)S(1)}, u32[]{:S(2)}, u32[]{:S(2)}) collective-permute-start(bf16[512,8,128]{2,1,0:T(8,128)(2,1)S(1)} %slice.8), channel_id=1, source_target_pairs={{0,4},{4,0},{8,12},{12,8},{16,20},{20,16},{24,28},{28,24},{32,36},... | collective-permute-start | bytes 3145736 | tf_op jit(solution)/shard_map/ppermute | solution.py:484
  131.7 2.2 %copy-start.1 = (bf16[512,32,128]{2,1,0:T(8,128)(2,1)S(1)}, bf16[512,32,128]{2,1,0:T(8,128)(2,1)}, u32[]{:S(2)}) copy-start(bf16[512,32,128]{2,1,0:T(8,128)(2,1)} %copy-done) | copy-start | bytes 12582916
  133.9 80.6 %copy-start.2 = (s32[128,1]{0,1:T(1,128)S(1)}, s32[128,1]{0,1:T(1,128)}, u32[]{:S(2)}) copy-start(s32[128,1]{0,1:T(1,128)} %param.9) | copy-start | bytes 1540
  149.6 64.9 %all-to-all-start.3 = ((bf16[512,16,128]{2,1,0:T(8,128)(2,1)}), bf16[512,16,128]{2,1,0:T(8,128)(2,1)}, u32[]{:S(2)}, u32[]{:S(2)}) async-start(bf16[512,16,128]{2,1,0:T(8,128)(2,1)} %get-tuple-element.29), calls=%async_computation.3 | async-start | bytes 4194304 | tf_op jit(solution)/shard_map/all_to_all | solution.py:476

commit v7 on v6

--- a/solution.py
+++ b/solution.py
@@ -19,6 +19,7 @@
 SOURCES = QBLK // MOST
 CHUNK = 16
 VMEM = 56 * 1024 * 1024
+ALL_VMEM = 63 * 1024 * 1024
 PAIR = 2
 POOL = PAIR * SHARE
 EXTRA = 5
@@ -428,9 +429,25 @@
             part,
             pltpu.VMEM((SOURCES // CHUNK, SHARE * CHUNK, HEAD), F32),
         ],
-        compiler_params=pltpu.CompilerParams(vmem_limit_bytes=VMEM // 2),
+        compiler_params=pltpu.CompilerParams(vmem_limit_bytes=ALL_VMEM),
         name="lean_attend",
     )(side, received, other)
+
+
+def tail_kernel(in_ref, out_ref):
+    out_ref[...] = in_ref[...].astype(F32)[:, HALF:, :].astype(BF16)
+
+
+def tails_of(received):
+    return pl.pallas_call(
+        tail_kernel,
+        grid=(PAIR,),
+        in_specs=[pl.BlockSpec((DEVICES // PAIR, TAIL, HEAD), lambda b: (b, 1, 0))],
+        out_specs=pl.BlockSpec((DEVICES // PAIR, HALF, HEAD), lambda b: (b, 0, 0)),
+        out_shape=jax.ShapeDtypeStruct((DEVICES, HALF, HEAD), BF16),
+        compiler_params=pltpu.CompilerParams(vmem_limit_bytes=ALL_VMEM),
+        name="tails",
+    )(received)
 
 
 def lean_unpack_kernel(row_ref, in_ref, out_ref, onehot_scr):
@@ -467,7 +484,7 @@
         out_specs=pl.BlockSpec((TOK, WIDE * HEAD), lambda g: (0, g)),
         out_shape=jax.ShapeDtypeStruct((TOK, HEADS * HEAD), BF16),
         scratch_shapes=[pltpu.VMEM((CLUSTERS // SHARE * UNIT, TOK), BF16)],
-        compiler_params=pltpu.CompilerParams(vmem_limit_bytes=63 * 1024 * 1024),
+        compiler_params=pltpu.CompilerParams(vmem_limit_bytes=ALL_VMEM),
         name="lean_unpack",
     )(row, back)
 
@@ -481,7 +498,7 @@
     sent = lean_pack(row, queries, keys, values)
     received = exchange(sent.reshape(DEVICES, MESSAGE, HEAD))
     swap = [(i, i ^ 1) for i in range(CLUSTERS)]
-    other = lax.ppermute(received[:, 3 * SHARE :, :], "seq", swap)
+    other = lax.ppermute(tails_of(received), "seq", swap)
     side = (lax.axis_index("seq") % PAIR).astype(jnp.int32).reshape(1)
     mixed, flags = lean_attend(side, received, other)
     back = exchange(mixed)

time: 218 us -> 218 us (level)
  Pallas kernels: 23.6 us -> 27.3 us
  local copies, waits for them, and re-layouts: 4.85 us -> 1.27 us
    unnamed x6 -> x2, local copies, waits for them, and re-layouts: 4.13 us -> 0.01 us
    pallas_call x0 -> x1, Pallas kernels: none -> 2.42 us  [tails_of(): pl.pallas_call(tail_kernel, grid=(PAIR,), in_specs=[pl.BlockSpec((DEVICES...]
  transfers between devices with their start and end apart: 2 -> 2, of which waited for: 2 -> 2; matrix products, arithmetic and copies ran while one was open for 0% -> 1% of each run, Pallas kernels for 0% -> 0%
where the time goes in v7:
time: 218 us; the launch traced here: 217 us
  blocking collectives  120 us (55%)
  waiting for transfers between devices  52.7 us (24%)
  Pallas kernels  27.3 us (13%)
  starting transfers between devices  15.5 us (7%)
    all_to_all x1, blocking collectives, exchange(): lax.all_to_all(data, ('seq', 'blk'), split_axis=0, concat_axis=0, tiled=T...  120 us
    all_to_all x1, waiting for transfers between devices, exchange(): lax.all_to_all(data, ('seq', 'blk'), split_axis=0, concat_axis=0, tiled=T...  50.1 us
    pallas_call x1, Pallas kernels, lean_attend(): pl.pallas_call(lean_attend_kernel, grid=(ROWS // QBLK,), in_specs=[pl.Blo...  17 us
    all_to_all x1, starting transfers between devices, exchange(): lax.all_to_all(data, ('seq', 'blk'), split_axis=0, concat_axis=0, tiled=T...  13 us
    pallas_call x1, Pallas kernels, lean_pack(): pl.pallas_call(lean_pack_kernel, grid=(HEADS // WIDE,), in_specs=[pl.Bloc...  4.98 us
  transfers between devices with their start and end apart: 2, of which 2 were waited for; matrix products, arithmetic and copies ran while one was open for 1% of the time, Pallas kernels for 0%

profile of v7, /device:TPU:1, one launch (start us, length us, event | category | flops | bytes accessed | tf_op | source)
XLA Modules:
  0.0 217.3 jit_solution(16985059300742637596)
XLA Ops:
  0.0 5.0 %lean_pack.1 = bf16[8,8,2,4,32,128]{5,4,3,2,1,0:T(8,128)(2,1)} custom-call(s32[1,128]{1,0:T(1,128)} %bitcast.10, bf16[128,4096]{1,0:T(8,128)(2,1)} %q_ref.1, bf16[128,4096]{1,0:T(8,128)(2,1)} %k_ref.1, bf16[128,4096]{1,0:T(8,128)(2,1)} %v_ref.1), custom_call_target="tpu_custom_call" | custom-call | tf_op jit(solution)/shard_map/lean_pack/pallas_call | solution.py:288
  5.0 119.9 %all_to_all.20.in_ref = bf16[512,32,128]{2,1,0:T(8,128)(2,1)} all-to-all(bf16[512,32,128]{2,1,0:T(8,128)(2,1)} %bitcast.8), channel_id=1, replica_groups=mesh['seq'=128,'blk'=4] {'seq','blk'}, dimensions={0} | all-to-all | bytes 8388608 | tf_op jit(solution)/shard_map/all_to_all | solution.py:493
  124.9 2.4 %tails.1 = bf16[512,8,128]{2,1,0:T(8,128)(2,1)} custom-call(bf16[512,32,128]{2,1,0:T(8,128)(2,1)} %all_to_all.20.in_ref), custom_call_target="tpu_custom_call" | custom-call | tf_op jit(solution)/shard_map/tails/pallas_call | solution.py:442
  127.3 2.6 %collective-permute-start = (bf16[512,8,128]{2,1,0:T(8,128)(2,1)}, bf16[512,8,128]{2,1,0:T(8,128)(2,1)}, u32[]{:S(2)}, u32[]{:S(2)}) collective-permute-start(bf16[512,8,128]{2,1,0:T(8,128)(2,1)} %tails.1), channel_id=1, source_target_pairs={{0,4},{4,0},{8,12},{12,8},{16,20},{20,16},{24,28},{28,24},{32,36},... | collective-permute-start | bytes 3145736 | tf_op jit(solution)/shard_map/ppermute | solution.py:501
  129.9 2.6 %collective-permute-done.other_ref = bf16[512,8,128]{2,1,0:T(8,128)(2,1)} collective-permute-done((bf16[512,8,128]{2,1,0:T(8,128)(2,1)}, bf16[512,8,128]{2,1,0:T(8,128)(2,1)}, u32[]{:S(2)}, u32[]{:S(2)}) %collective-permute-start) | collective-permute-done | bytes 1048608 | tf_op jit(solution)/shard_map/ppermute | solution.py:501
  132.5 0.0 copy-start
  132.5 17.0 %lean_attend.1 = (bf16[512,16,128]{2,1,0:T(8,128)(2,1)}, f32[8,128]{1,0:T(8,128)}) custom-call(s32[1]{0:T(128)} %bitcast.3.side_ref, bf16[512,32,128]{2,1,0:T(8,128)(2,1)} %all_to_all.20.in_ref, bf16[512,8,128]{2,1,0:T(8,128)(2,1)} %collective-permute-done.other_ref), custom_call_target="tpu_custom_call" | custom-call | tf_op jit(solution)/shard_map/lean_attend/pallas_call | solution.py:409
  149.6 13.0 %all-to-all-start.3 = ((bf16[512,16,128]{2,1,0:T(8,128)(2,1)}), bf16[512,16,128]{2,1,0:T(8,128)(2,1)}, u32[]{:S(2)}, u32[]{:S(2)}) async-start(bf16[512,16,128]{2,1,0:T(8,128)(2,1)} %get-tuple-element.29), calls=%async_computation.3 | async-start | bytes 4194304 | tf_op jit(solution)/shard_map/all_to_all | solution.py:493
  162.5 1.3 slice.3
  164.4 50.1 %all-to-all-done.3 = bf16[512,16,128]{2,1,0:T(8,128)(2,1)} async-done(((bf16[512,16,128]{2,1,0:T(8,128)(2,1)}), bf16[512,16,128]{2,1,0:T(8,128)(2,1)}, u32[]{:S(2)}, u32[]{:S(2)}) %all-to-all-start.3) | async-done | bytes 2097184 | tf_op jit(solution)/shard_map/all_to_all | solution.py:493
  214.4 0.0 copy-done
  214.4 2.9 %conditional.1 = (bf16[128,4096]{1,0:T(8,128)(2,1)}) conditional(s32[]{:T(128)} %bitcast.6, (bf16[512,16,128]{2,1,0:T(8,128)(2,1)}, s32[1,128]{1,0:T(1,128)S(1)}) %tuple.17, (s32[1,128]{1,0:T(1,128)S(1)}, bf16[128,4096]{1,0:T(8,128)(2,1)}, bf16[128,4096]{1,0:T(8,128)(2,1)}, bf16[128,4096]{1,0:T(8,128)(2,1)}) %tuple.18), branch_computations={%region_0.1_spmd, %region_1.2_spmd} | conditional | bytes 16777224 | solution.py:516
  214.4 2.9 %lean_unpack.1 = bf16[128,4096]{1,0:T(8,128)(2,1)} custom-call(s32[1,128]{1,0:T(1,128)S(1)} %get-tuple-element.20.row_ref, bf16[8,8,2,4,16,128]{5,4,3,2,1,0:T(8,128)(2,1)} %bitcast.in_ref), custom_call_target="tpu_custom_call" | custom-call | tf_op jit(solution)/shard_map/cond/branch_0_fun/lean_unpack/pallas_call | solution.py:477
Async XLA Ops:
  127.3 5.2 %collective-permute-start = (bf16[512,8,128]{2,1,0:T(8,128)(2,1)}, bf16[512,8,128]{2,1,0:T(8,128)(2,1)}, u32[]{:S(2)}, u32[]{:S(2)}) collective-permute-start(bf16[512,8,128]{2,1,0:T(8,128)(2,1)} %tails.1), channel_id=1, source_target_pairs={{0,4},{4,0},{8,12},{12,8},{16,20},{20,16},{24,28},{28,24},{32,36},... | collective-permute-start | bytes 3145736 | tf_op jit(solution)/shard_map/ppermute | solution.py:501
  132.5 81.9 %copy-start = (s32[128,1]{0,1:T(1,128)S(1)}, s32[128,1]{0,1:T(1,128)}, u32[]{:S(2)}) copy-start(s32[128,1]{0,1:T(1,128)} %param.9) | copy-start | bytes 1540
  149.6 64.9 %all-to-all-start.3 = ((bf16[512,16,128]{2,1,0:T(8,128)(2,1)}), bf16[512,16,128]{2,1,0:T(8,128)(2,1)}, u32[]{:S(2)}, u32[]{:S(2)}) async-start(bf16[512,16,128]{2,1,0:T(8,128)(2,1)} %get-tuple-element.29), calls=%async_computation.3 | async-start | bytes 4194304 | tf_op jit(solution)/shard_map/all_to_all | solution.py:493

commit v8 on v7

--- a/solution.py
+++ b/solution.py
@@ -435,7 +435,7 @@
 
 
 def tail_kernel(in_ref, out_ref):
-    out_ref[...] = in_ref[...].astype(F32)[:, HALF:, :].astype(BF16)
+    out_ref[...] = in_ref[:, HALF:, :]
 
 
 def tails_of(received):

time: 218 us -> 218 us (level)
  no operation moved by 1% of the time
where the time goes in v8:
time: 218 us; the launch traced here: 217 us
  blocking collectives  120 us (55%)
  waiting for transfers between devices  52.7 us (24%)
  Pallas kernels  27.3 us (13%)
  starting transfers between devices  15.5 us (7%)
    all_to_all x1, blocking collectives, exchange(): lax.all_to_all(data, ('seq', 'blk'), split_axis=0, concat_axis=0, tiled=T...  120 us
    all_to_all x1, waiting for transfers between devices, exchange(): lax.all_to_all(data, ('seq', 'blk'), split_axis=0, concat_axis=0, tiled=T...  50.1 us
    pallas_call x1, Pallas kernels, lean_attend(): pl.pallas_call(lean_attend_kernel, grid=(ROWS // QBLK,), in_specs=[pl.Blo...  17 us
    all_to_all x1, starting transfers between devices, exchange(): lax.all_to_all(data, ('seq', 'blk'), split_axis=0, concat_axis=0, tiled=T...  13 us
    pallas_call x1, Pallas kernels, lean_pack(): pl.pallas_call(lean_pack_kernel, grid=(HEADS // WIDE,), in_specs=[pl.Bloc...  4.98 us
  transfers between devices with their start and end apart: 2, of which 2 were waited for; matrix products, arithmetic and copies ran while one was open for 1% of the time, Pallas kernels for 0%

profile of v8, /device:TPU:1, one launch (start us, length us, event | category | flops | bytes accessed | tf_op | source)
XLA Modules:
  0.0 217.3 jit_solution(17066183380109433316)
XLA Ops:
  0.0 5.0 %lean_pack.1 = bf16[8,8,2,4,32,128]{5,4,3,2,1,0:T(8,128)(2,1)} custom-call(s32[1,128]{1,0:T(1,128)} %bitcast.10, bf16[128,4096]{1,0:T(8,128)(2,1)} %q_ref.1, bf16[128,4096]{1,0:T(8,128)(2,1)} %k_ref.1, bf16[128,4096]{1,0:T(8,128)(2,1)} %v_ref.1), custom_call_target="tpu_custom_call" | custom-call | tf_op jit(solution)/shard_map/lean_pack/pallas_call | solution.py:288
  5.0 119.9 %all_to_all.20.in_ref = bf16[512,32,128]{2,1,0:T(8,128)(2,1)} all-to-all(bf16[512,32,128]{2,1,0:T(8,128)(2,1)} %bitcast.8), channel_id=1, replica_groups=mesh['seq'=128,'blk'=4] {'seq','blk'}, dimensions={0} | all-to-all | bytes 8388608 | tf_op jit(solution)/shard_map/all_to_all | solution.py:493
  124.9 2.4 %tails.1 = bf16[512,8,128]{2,1,0:T(8,128)(2,1)} custom-call(bf16[512,32,128]{2,1,0:T(8,128)(2,1)} %all_to_all.20.in_ref), custom_call_target="tpu_custom_call" | custom-call | tf_op jit(solution)/shard_map/tails/pallas_call | solution.py:442
  127.3 2.6 %collective-permute-start = (bf16[512,8,128]{2,1,0:T(8,128)(2,1)}, bf16[512,8,128]{2,1,0:T(8,128)(2,1)}, u32[]{:S(2)}, u32[]{:S(2)}) collective-permute-start(bf16[512,8,128]{2,1,0:T(8,128)(2,1)} %tails.1), channel_id=1, source_target_pairs={{0,4},{4,0},{8,12},{12,8},{16,20},{20,16},{24,28},{28,24},{32,36},... | collective-permute-start | bytes 3145736 | tf_op jit(solution)/shard_map/ppermute | solution.py:501
  129.9 2.6 %collective-permute-done.other_ref = bf16[512,8,128]{2,1,0:T(8,128)(2,1)} collective-permute-done((bf16[512,8,128]{2,1,0:T(8,128)(2,1)}, bf16[512,8,128]{2,1,0:T(8,128)(2,1)}, u32[]{:S(2)}, u32[]{:S(2)}) %collective-permute-start) | collective-permute-done | bytes 1048608 | tf_op jit(solution)/shard_map/ppermute | solution.py:501
  132.5 0.0 copy-start
  132.5 17.0 %lean_attend.1 = (bf16[512,16,128]{2,1,0:T(8,128)(2,1)}, f32[8,128]{1,0:T(8,128)}) custom-call(s32[1]{0:T(128)} %bitcast.3.side_ref, bf16[512,32,128]{2,1,0:T(8,128)(2,1)} %all_to_all.20.in_ref, bf16[512,8,128]{2,1,0:T(8,128)(2,1)} %collective-permute-done.other_ref), custom_call_target="tpu_custom_call" | custom-call | tf_op jit(solution)/shard_map/lean_attend/pallas_call | solution.py:409
  149.6 13.0 %all-to-all-start.3 = ((bf16[512,16,128]{2,1,0:T(8,128)(2,1)}), bf16[512,16,128]{2,1,0:T(8,128)(2,1)}, u32[]{:S(2)}, u32[]{:S(2)}) async-start(bf16[512,16,128]{2,1,0:T(8,128)(2,1)} %get-tuple-element.29), calls=%async_computation.3 | async-start | bytes 4194304 | tf_op jit(solution)/shard_map/all_to_all | solution.py:493
  162.5 1.3 slice.3
  164.4 50.1 %all-to-all-done.3 = bf16[512,16,128]{2,1,0:T(8,128)(2,1)} async-done(((bf16[512,16,128]{2,1,0:T(8,128)(2,1)}), bf16[512,16,128]{2,1,0:T(8,128)(2,1)}, u32[]{:S(2)}, u32[]{:S(2)}) %all-to-all-start.3) | async-done | bytes 2097184 | tf_op jit(solution)/shard_map/all_to_all | solution.py:493
  214.4 0.0 copy-done
  214.4 2.9 %conditional.1 = (bf16[128,4096]{1,0:T(8,128)(2,1)}) conditional(s32[]{:T(128)} %bitcast.6, (bf16[512,16,128]{2,1,0:T(8,128)(2,1)}, s32[1,128]{1,0:T(1,128)S(1)}) %tuple.17, (s32[1,128]{1,0:T(1,128)S(1)}, bf16[128,4096]{1,0:T(8,128)(2,1)}, bf16[128,4096]{1,0:T(8,128)(2,1)}, bf16[128,4096]{1,0:T(8,128)(2,1)}) %tuple.18), branch_computations={%region_0.1_spmd, %region_1.2_spmd} | conditional | bytes 16777224 | solution.py:516
  214.4 2.9 %lean_unpack.1 = bf16[128,4096]{1,0:T(8,128)(2,1)} custom-call(s32[1,128]{1,0:T(1,128)S(1)} %get-tuple-element.20.row_ref, bf16[8,8,2,4,16,128]{5,4,3,2,1,0:T(8,128)(2,1)} %bitcast.in_ref), custom_call_target="tpu_custom_call" | custom-call | tf_op jit(solution)/shard_map/cond/branch_0_fun/lean_unpack/pallas_call | solution.py:477
Async XLA Ops:
  127.3 5.2 %collective-permute-start = (bf16[512,8,128]{2,1,0:T(8,128)(2,1)}, bf16[512,8,128]{2,1,0:T(8,128)(2,1)}, u32[]{:S(2)}, u32[]{:S(2)}) collective-permute-start(bf16[512,8,128]{2,1,0:T(8,128)(2,1)} %tails.1), channel_id=1, source_target_pairs={{0,4},{4,0},{8,12},{12,8},{16,20},{20,16},{24,28},{28,24},{32,36},... | collective-permute-start | bytes 3145736 | tf_op jit(solution)/shard_map/ppermute | solution.py:501
  132.5 81.9 %copy-start = (s32[128,1]{0,1:T(1,128)S(1)}, s32[128,1]{0,1:T(1,128)}, u32[]{:S(2)}) copy-start(s32[128,1]{0,1:T(1,128)} %param.9) | copy-start | bytes 1540
  149.6 64.9 %all-to-all-start.3 = ((bf16[512,16,128]{2,1,0:T(8,128)(2,1)}), bf16[512,16,128]{2,1,0:T(8,128)(2,1)}, u32[]{:S(2)}, u32[]{:S(2)}) async-start(bf16[512,16,128]{2,1,0:T(8,128)(2,1)} %get-tuple-element.29), calls=%async_computation.3 | async-start | bytes 4194304 | tf_op jit(solution)/shard_map/all_to_all | solution.py:493
